TPU v7x, 256 devices: a whole 4x4x8 slice. The times are simulated.
256 devices in a mesh: feat: 16 (over x_lo, z), dp: 16 (over y, x_hi, core).
Axes of the slice: x: 4 (x_hi: 2, x_lo: 2; x = x_hi * 2 + x_lo), y: 4, z: 8, core: 2. Of those that a mesh axis runs over, the one named last changes fastest.
Arguments:
- node_feats: bfloat16 [16, 6144, 1024], P('dp', None, 'feat'), may hold values from -6 to 6
- target_ids: int32 [16, 1536], P('dp'), may hold values from 0 to 6143
- layer_one_nbrs: int32 [16, 1536, 10], P('dp'), may hold values from 0 to 6143
- layer_one_counts: int32 [16, 1536], P('dp'), may hold values from 1 to 10
- layer_two_nbrs: int32 [16, 256, 5], P('dp', 'feat'), may hold values from 0 to 95
- layer_two_counts: int32 [16, 256], P('dp', 'feat'), may hold values from 1 to 5
- labels: int32 [16, 256], P('dp', 'feat'), may hold values from 0 to 18
- layer_one_weight: bfloat16 [2, 1024, 1024], P(None, 'feat'), may hold values from -0.1875 to 0.1875
- layer_two_weight: bfloat16 [2, 1024, 1024], replicated, may hold values from -0.1875 to 0.1875
- head_weight: bfloat16 [1024, 19], replicated, may hold values from -0.1875 to 0.1875
Outputs:
- hidden: bfloat16 [16, 1536, 1024], P('dp', 'feat')
- logits: float32 [16, 256, 19], P('dp', 'feat')
- grad_one: float32 [2, 1024, 1024], P(None, 'feat', 'dp')
- grad_two: float32 [2, 1024, 1024], P(None, 'feat', 'dp')
- grad_head: float32 [1024, 19], P('feat')
Inputs may be any that keep to these rules, and one draw needn't show every extreme that they name: `target_ids`: rows of the micro-batch's sampled nodes. `layer_one_nbrs`: slots past a row's count are padding and are ignored. `layer_two_nbrs`: rows of the seed owner's block of 96 layer-one rows; slots past the seed's count are padding and are ignored.
All inputs are finite; a program needn't handle non-finite values.
Results may differ from a plain program's by a relative error of at most 0.03.
Values may be sent and summed in bfloat16 or wider, within the bound.
A program may use at most 128 MiB of HBM per device.

v0:
```python
import jax
import jax.numpy as jnp
from jax import lax
from jax.sharding import PartitionSpec as P


def silu_slope(values):
    sigma = jax.nn.sigmoid(values)
    return sigma + values * sigma * (1.0 - sigma)


def shards(
    node_feats,
    target_ids,
    layer_one_nbrs,
    layer_one_counts,
    layer_two_nbrs,
    layer_two_counts,
    labels,
    layer_one_weight,
    layer_two_weight,
    head_weight,
):
    features = node_feats[0]
    feat_size = lax.axis_size("feat")
    self_rows = jnp.take(features, target_ids[0], axis=0)
    one_counts = layer_one_counts[0]
    valid_one = jnp.arange(layer_one_nbrs.shape[2])[None, :] < one_counts[:, None]
    picked_one = jnp.take(features, layer_one_nbrs[0], axis=0)
    summed_one = jnp.sum(
        jnp.where(valid_one[:, :, None], picked_one, jnp.zeros((), jnp.bfloat16)),
        axis=1,
        dtype=jnp.float32,
    )
    mean_rows = (summed_one / one_counts[:, None].astype(jnp.float32)).astype(jnp.bfloat16)
    hidden_rows = self_rows.shape[0] // feat_size
    part_self = self_rows
    part_mean = mean_rows
    pre_act = lax.psum_scatter(
        (
            jnp.dot(part_self, layer_one_weight[0], preferred_element_type=jnp.float32)
            + jnp.dot(part_mean, layer_one_weight[1], preferred_element_type=jnp.float32)
        ).astype(jnp.bfloat16),
        "feat",
        scatter_dimension=0,
        tiled=True,
    ).astype(jnp.float32)
    hidden = jax.nn.silu(pre_act).astype(jnp.bfloat16)
    seed_count = layer_two_nbrs.shape[1]
    fan_two = layer_two_nbrs.shape[2]
    two_nbrs = layer_two_nbrs[0]
    two_counts = layer_two_counts[0]
    seed_hidden = hidden[:seed_count]
    valid_two = jnp.arange(fan_two)[None, :] < two_counts[:, None]
    count_float = two_counts.astype(jnp.float32)
    picked_two = jnp.take(hidden, two_nbrs, axis=0)
    summed_two = jnp.sum(
        jnp.where(valid_two[:, :, None], picked_two, jnp.zeros((), jnp.bfloat16)),
        axis=1,
        dtype=jnp.float32,
    )
    neigh_mean = (summed_two / count_float[:, None]).astype(jnp.bfloat16)
    upper_pre = jnp.dot(
        seed_hidden, layer_two_weight[0], preferred_element_type=jnp.float32
    ) + jnp.dot(neigh_mean, layer_two_weight[1], preferred_element_type=jnp.float32)
    upper_hidden = jax.nn.silu(upper_pre).astype(jnp.bfloat16)
    logits = jnp.dot(upper_hidden, head_weight, preferred_element_type=jnp.float32)
    classes = head_weight.shape[1]
    probability = jax.nn.softmax(logits, axis=-1)
    one_hot = (labels[0][:, None] == jnp.arange(classes)[None, :]).astype(jnp.float32)
    grad_logits = ((probability - one_hot) / float(seed_count * feat_size)).astype(jnp.bfloat16)
    grad_head = jnp.einsum(
        "sh,sc->hc", upper_hidden, grad_logits, preferred_element_type=jnp.float32
    )
    back_hidden = jnp.einsum(
        "sc,hc->sh", grad_logits, head_weight, preferred_element_type=jnp.float32
    )
    grad_upper = (back_hidden * silu_slope(upper_pre)).astype(jnp.bfloat16)
    grad_two = jnp.stack(
        [
            jnp.einsum("sh,sk->hk", seed_hidden, grad_upper, preferred_element_type=jnp.float32),
            jnp.einsum("sh,sk->hk", neigh_mean, grad_upper, preferred_element_type=jnp.float32),
        ]
    )
    back_seed = jnp.einsum(
        "sk,hk->sh", grad_upper, layer_two_weight[0], preferred_element_type=jnp.float32
    )
    back_mean = jnp.einsum(
        "sk,hk->sh", grad_upper, layer_two_weight[1], preferred_element_type=jnp.float32
    )
    slot_weight = jnp.where(valid_two, 1.0 / count_float[:, None], 0.0)
    matches = (two_nbrs[:, :, None] == jnp.arange(hidden_rows)[None, None, :]).astype(jnp.float32)
    spread_table = jnp.sum(slot_weight[:, :, None] * matches, axis=1)
    back_rows = jnp.einsum("sr,sh->rh", spread_table, back_mean, precision=lax.Precision.HIGHEST)
    back_rows = back_rows + jnp.pad(back_seed, ((0, hidden_rows - seed_count), (0, 0)))
    grad_pre = (back_rows * silu_slope(pre_act)).astype(jnp.bfloat16)
    piece = lax.all_gather(grad_pre, "feat", axis=0, tiled=True)
    part_self = self_rows
    part_mean = mean_rows
    grad_local = jnp.stack(
        [
            jnp.einsum("rc,rh->ch", part_self, piece, preferred_element_type=jnp.float32),
            jnp.einsum("rc,rh->ch", part_mean, piece, preferred_element_type=jnp.float32),
        ]
    )
    grad_one = lax.psum_scatter(
        grad_local.astype(jnp.bfloat16), "dp", scatter_dimension=2, tiled=True
    ).astype(jnp.float32)
    two_part, head_part = (
        lax.psum_scatter(
            grad_two.astype(jnp.bfloat16), "feat", scatter_dimension=1, tiled=True
        ).astype(jnp.float32),
        lax.psum_scatter(
            grad_head.astype(jnp.bfloat16), "feat", scatter_dimension=0, tiled=True
        ).astype(jnp.float32),
    )
    grad_two_out = lax.psum_scatter(
        two_part.astype(jnp.bfloat16), "dp", scatter_dimension=2, tiled=True
    ).astype(jnp.float32)
    grad_head_out = lax.psum(head_part, "dp")
    return (hidden[None], logits[None], grad_one, grad_two_out, grad_head_out)


def solution(mesh):
    return jax.shard_map(
        shards,
        mesh=mesh,
        in_specs=(
            P("dp", None, "feat"),
            P("dp", None),
            P("dp", None, None),
            P("dp", None),
            P("dp", "feat", None),
            P("dp", "feat"),
            P("dp", "feat"),
            P(None, "feat", None),
            P(),
            P(),
        ),
        out_specs=(
            P("dp", "feat", None),
            P("dp", "feat", None),
            P(None, "feat", "dp"),
            P(None, "feat", "dp"),
            P("feat", None),
        ),
        check_vma=False,
    )
```

profile of v0, /device:TPU:1, one launch (start us, length us, event | category | flops | bytes accessed | tf_op | source)
XLA Modules:
  0.0 561.3 jit_solution(12561141592532440374)
XLA Ops:
  12.7 1.8 copy.32
  14.5 3.2 gather_fusion
  17.7 53.9 %gather_fusion.1 = bf16[15360,64]{1,0:T(8,128)(2,1)} fusion(bf16[6144,64]{1,0:T(8,128)(2,1)S(1)} %bitcast.74, s32[15360]{0:T(1024)S(1)} %broadcast_clamp_fusion), kind=kCustom, calls=%fused_computation.1 | custom fusion | bytes 3993600 | tf_op jit(solution)/shard_map/jit(_take)/gather | solution.py:29
  71.7 8.5 %reshape.226 = bf16[1536,10,64]{2,1,0:T(8,128)(2,1)} reshape(bf16[15360,64]{1,0:T(8,128)(2,1)} %gather_fusion.1) | data formatting | bytes 3932160 | tf_op jit(solution)/shard_map/jit(_take)/gather | solution.py:29
  80.1 10.4 %convert_reduce_fusion = f32[1536,64]{1,0:T(8,128)S(1)} fusion(bf16[1536,10,64]{2,1,0:T(8,128)(2,1)} %reshape.226, pred[1536,10]{1,0:T(8,128)(4,1)S(1)} %copy.33, pred[1536,10]{1,0:T(8,128)(4,1)S(1)} %iota_compare_fusion), kind=kLoop, calls=%fused_computation.3 | loop fusion | flops 3833856 | bytes 2390016 | tf_op jit(solution)/shard_map/reduce_sum | solution.py:30
  90.5 1.0 fusion.24
  91.6 2.7 add_convert_fusion
  95.0 70.8 %reduce-scatter.12.cloned.1.call-done = bf16[96,1024]{1,0:T(8,128)(2,1)} async-done(((bf16[1536,1024]{1,0:T(8,128)(2,1)}), bf16[96,1024]{1,0:T(8,128)(2,1)}) %reduce-scatter.12.cloned.1.call-update) | async-done | bytes 196624 | tf_op jit(solution)/shard_map/reduce_scatter | solution.py:39
  165.8 1.0 fusion.23
  168.0 2.2 fusion.2
  170.2 2.0 fusion.30
  174.2 1.3 fusion.13
  177.1 2.3 pad_maximum_fusion
  180.7 67.0 %all-gather.2.cloned.1.call-done = bf16[1536,1024]{1,0:T(8,128)(2,1)} async-done(((bf16[96,1024]{1,0:T(8,128)(2,1)}), bf16[1536,1024]{1,0:T(8,128)(2,1)}) %all-gather.2.cloned.1.call-update) | async-done | bytes 3145744 | tf_op jit(solution)/shard_map/all_gather | solution.py:97
  247.7 3.0 fusion.15
  250.8 0.9 fusion.14
  252.2 0.9 reshape.243
  253.2 73.4 %reduce-scatter.14.cloned.1.call-done = bf16[2,64,1024]{2,1,0:T(8,128)(2,1)} async-done(((bf16[2,1024,1024]{2,1,0:T(8,128)(2,1)}), bf16[2,64,1024]{2,1,0:T(8,128)(2,1)}) %reduce-scatter.14.cloned.1.call-update) | async-done | bytes 262160 | tf_op jit(solution)/shard_map/reduce_scatter | solution.py:110
  326.6 1.3 copy.40
  327.8 0.9 reshape.245
  329.6 63.7 %reduce-scatter.20.cloned.1.call-done = bf16[64,19]{1,0:T(8,128)(2,1)} async-done(((bf16[1024,19]{1,0:T(8,128)(2,1)}), bf16[64,19]{1,0:T(8,128)(2,1)}) %reduce-scatter.20.cloned.1.call-update) | async-done | bytes 2448
  394.1 71.8 %psum.7 = f32[64,19]{0,1:T(8,128)} all-reduce(bf16[64,19]{0,1:T(8,128)(2,1)S(1)} %copy.43), channel_id=1, replica_groups=mesh['feat'=16,'dp'=16] {'dp'}, use_global_device_ids=true, to_apply=%region_10.11 | all-reduce | flops 1216 | bytes 7296 | tf_op jit(solution)/shard_map/psum | solution.py:120
  466.0 10.8 %reduce-scatter.16.cloned.1.call-done = bf16[64,128]{1,0:T(8,128)(2,1)} async-done(((bf16[1024,128]{1,0:T(8,128)(2,1)}), bf16[64,128]{1,0:T(8,128)(2,1)}) %reduce-scatter.16.cloned.1.call-update) | async-done | bytes 16400
  478.3 74.6 %reduce-scatter.18.cloned.1.call-done = bf16[64,128]{1,0:T(8,128)(2,1)} async-done(((bf16[1024,128]{1,0:T(8,128)(2,1)}), bf16[64,128]{1,0:T(8,128)(2,1)}) %reduce-scatter.18.cloned.1.call-update) | async-done | bytes 16400
  (78 shorter events, 17.3 us)
Async XLA Ops:
  7.2 165.1 %copy-start = (bf16[1024,19]{0,1:T(8,128)(2,1)S(1)}, bf16[1024,19]{0,1:T(8,128)(2,1)}, u32[]{:S(2)}) copy-start(bf16[1024,19]{0,1:T(8,128)(2,1)} %param.19) | copy-start | bytes 116740
  7.2 158.6 %reduce-scatter.12.cloned.1.call-start = ((), (), s32[]{:S(2)}) async-start(), calls=%async_computation.5 | async-start | bytes 3342336 | tf_op jit(solution)/shard_map/reduce_scatter | solution.py:39
  80.1 10.4 %copy-start.4 = (bf16[2,64,1024]{2,1,0:T(8,128)(2,1)S(1)}, bf16[2,64,1024]{2,1,0:T(8,128)(2,1)}, u32[]{:S(2)}) copy-start(bf16[2,64,1024]{2,1,0:T(8,128)(2,1)} %param.17) | copy-start | bytes 786436
  91.6 2.8 copy-start.6
  91.6 3.1 copy-start.7
  94.3 153.4 %all-gather.2.cloned.1.call-start = ((), (), s32[]{:S(2)}) async-start(), calls=%async_computation.6 | async-start | bytes 3342336 | tf_op jit(solution)/shard_map/all_gather | solution.py:97
  166.9 5.8 %copy-start.8 = (s32[1,16]{1,0:T(1,128)S(1)}, s32[1,16]{1,0:T(1,128)}, u32[]{:S(2)}) copy-start(s32[1,16]{1,0:T(1,128)} %param.16) | copy-start | bytes 196
  167.7 5.2 copy-start.1
  170.2 4.0 copy-start.3
  172.5 7.0 %copy-start.5 = (f32[16,19]{1,0:T(8,128)}, f32[16,19]{1,0:T(8,128)S(1)}, u32[]{:S(2)}) copy-start(f32[16,19]{1,0:T(8,128)S(1)} %get-tuple-element.8) | copy-start | bytes 3652
  175.5 151.1 %reduce-scatter.14.cloned.1.call-start = ((), (), s32[]{:S(2)}) async-start(), calls=%async_computation.7 | async-start | bytes 4456448 | tf_op jit(solution)/shard_map/reduce_scatter | solution.py:110
  179.4 213.9 %reduce-scatter.20.cloned.1.call-start = ((), (), s32[]{:S(2)}) async-start(), calls=%async_computation.10 | async-start | bytes 278528
  180.6 296.1 %reduce-scatter.16.cloned.1.call-start = ((), (), s32[]{:S(2)}) async-start(), calls=%async_computation.8 | async-start | bytes 278528
  247.7 3.0 copy-start.2
  253.1 299.8 %reduce-scatter.18.cloned.1.call-start = ((), (), s32[]{:S(2)}) async-start(), calls=%async_computation.9 | async-start | bytes 278528
Sparse Core Ops, SparseCore 0:
  94.4 71.3 reduce-scatter.11
  175.6 72.0 all-gather.1
  250.3 76.2 reduce-scatter.13
  328.9 64.3 reduce-scatter.19
  397.7 79.0 reduce-scatter.15
  481.1 71.7 reduce-scatter.17
where the time goes:
time: 563 us; the launch traced here: 561 us
  waiting for transfers between devices  360 us (64%)
  local copies, waits for them, and re-layouts  76.8 us (14%)
  blocking collectives  71.8 us (13%)
  other arithmetic  20.8 us (4%)
  matrix products  16.7 us (3%)
  between operations  14.4 us (3%)
    unnamed x9, waiting for transfers between devices  149 us
    reduce_scatter x1, waiting for transfers between devices, shards(): lax.psum_scatter(grad_two.astype(jnp.bfloat16), 'feat', scatter_dimension...  73.4 us
    psum x1, blocking collectives, shards(): grad_head_out = lax.psum(head_part, 'dp')  71.8 us
    reduce_scatter x1, waiting for transfers between devices, shards(): lax.psum_scatter((jnp.dot(part_self, layer_one_weight[0], preferred_eleme...  70.8 us
    all_gather x1, waiting for transfers between devices, shards(): piece = lax.all_gather(grad_pre, 'feat', axis=0, tiled=True)  67 us
    gather x2, local copies, waits for them, and re-layouts, shards(): picked_one = jnp.take(features, layer_one_nbrs[0], axis=0)  62.4 us
  transfers between devices with their start and end apart: 6, of which 6 were waited for; matrix products, arithmetic and copies ran while one was open for 3% of the time, Pallas kernels for 0%

commit v1 on v0

v1 whole, which is shorter than its diff:
```python
import functools

import jax
import jax.numpy as jnp
from jax import lax
from jax.experimental import pallas as pl
from jax.experimental.pallas import tpu as pltpu
from jax.sharding import PartitionSpec as P

MESH = pl.DeviceIdType.MESH
BF16 = jnp.bfloat16
F32 = jnp.float32

NODES = 6144
ROWS = 96
SEEDS = 16
FAN1 = 10
FAN2 = 5
CLASSES = 19
WIDE = 1024
TN = (((0,), (0,)), ((), ()))
NT = (((1,), (1,)), ((), ()))


def sigmoid(values):
    return 1.0 / (1.0 + jnp.exp(-values))


def silu_slope(values):
    sigma = sigmoid(values)
    return sigma + values * sigma * (1.0 - sigma)


def kernel(
    idx_ref, inv_ref, feats_hbm, w1_hbm, w2_hbm, head_ref, nbr_ref, cnt_ref, lab_ref,
    hidden_ref, logits_ref, one_ref, two_ref, ghead_ref,
    feats, tab, rows, a4, a_full, w1, w2, headp, pre, p_send, p_recv, g_send, g_recv, z_send, z_recv, hd_send, hd_recv,
    load_sem, wa_s, wa_r, wb_s, wb_r, wc_s, wc_r, m1_s, m1_r, mq_s, mq_r, m2_s, m2_r, m3_s, m3_r, m4_s, m4_r, m5_s, m5_r,
):
    f = lax.axis_index("feat")
    d = lax.axis_index("dp")
    xl, z = f // 8, f % 8
    y, xh, c = d // 4, (d // 2) % 2, d % 2
    quad = z // 2
    mine = xl * 2 + z % 2

    def feat_at(r):
        return ((xl + r // 8) % 2) * 8 + (z + r % 8) % 8

    def feat_from(r):
        return ((xl + r // 8) % 2) * 8 + (z + 8 - r % 8) % 8

    def dp_at(r):
        return (d + r) % 16

    def send(src, dst, ss, rs, **where):
        return pltpu.make_async_remote_copy(
            src_ref=src, dst_ref=dst, send_sem=ss, recv_sem=rs, device_id=where, device_id_type=MESH
        )

    def loop(lo, hi, fn):
        def body(i, carry):
            fn(i)
            return carry

        lax.fori_loop(lo, hi, body, 0)

    feat_load = pltpu.make_async_copy(feats_hbm, feats, load_sem.at[0])
    feat_load.start()
    w2_load = pltpu.make_async_copy(w2_hbm, w2, load_sem.at[1])
    w2_load.start()
    w1_load = pltpu.make_async_copy(w1_hbm.at[y, c], w1.at[f, y, c], load_sem.at[2])
    w1_load.start()

    barrier = pltpu.get_barrier_semaphore()

    def greet(r):
        pl.semaphore_signal(barrier, inc=1, device_id={"feat": feat_at(r)}, device_id_type=MESH)
        pl.semaphore_signal(barrier, inc=1, device_id={"dp": dp_at(r)}, device_id_type=MESH)

    loop(1, 16, greet)

    headp[...] = jnp.zeros_like(headp)
    headp[:, 0:CLASSES] = head_ref[...]

    feat_load.wait()

    def widen(i):
        part = feats[pl.ds(i * 256, 256), :].astype(F32)
        tab[pl.ds(i * 256, 256), :] = jnp.concatenate([part, part], axis=1)

    loop(0, NODES // 256, widen)
    tab[pl.ds(NODES, 8), :] = jnp.zeros((8, 128), F32)

    w1_load.wait()
    pl.semaphore_wait(barrier, 30)

    def wa(r):
        return send(w1.at[f, y, c], w1.at[f, y, c], wa_s.at[r], wa_r.at[r], feat=feat_at(r))

    loop(1, 16, lambda r: wa(r).start())

    def wb(h, r):
        half = (xl + h) % 2
        spot = w1.at[pl.ds(half * 8, 8), y, c]
        return send(spot, spot, wb_s.at[h, r], wb_r.at[h, r], dp=((y + r) % 4) * 4 + xh * 2 + c)

    def wc(h):
        half = (xl + h) % 2
        spot = w1.at[pl.ds(half * 8, 8), :, c]
        return send(spot, spot, wc_s.at[h], wc_r.at[h], dp=y * 4 + xh * 2 + 1 - c)

    lane = lax.broadcasted_iota(jnp.int32, (1, 128), 1)
    left = lane < 64

    def gather(k):
        def body(g):
            for u in range(8):
                local = g * 8 + u
                t = k * ROWS + local
                vals = [tab[pl.ds(idx_ref[j, t], 1), :] for j in range(FAN1 + 1)]
                total = vals[1:]
                while len(total) > 1:
                    total = [
                        total[i] + total[i + 1] if i + 1 < len(total) else total[i]
                        for i in range(0, len(total), 2)
                    ]
                rows[pl.ds(local, 1), :] = jnp.where(left, vals[0], total[0] * inv_ref[0, t])

        loop(0, ROWS // 8, body)
        a4[mine, k] = rows[...].astype(BF16)

    lanes_f = pl.ds(pl.multiple_of(f * 128, 128), 128)

    def m1(r):
        return send(a4.at[mine, feat_at(r)], a_full.at[:, lanes_f], m1_s.at[r], m1_r.at[r], feat=feat_at(r))

    def block(r):
        gather(feat_at(r))
        m1(r).start()

        @pl.when(r == 5)
        def _():
            loop(1, 8, lambda i: wa(i).wait_recv())
            loop(1, 4, lambda i: wb(0, i).start())

        @pl.when(r == 8)
        def _():
            loop(8, 16, lambda i: wa(i).wait_recv())
            loop(1, 4, lambda i: wb(1, i).start())

        @pl.when(r == 12)
        def _():
            loop(1, 4, lambda i: wb(0, i).wait_recv())
            wc(0).start()

        @pl.when(r == 15)
        def _():
            loop(1, 4, lambda i: wb(1, i).wait_recv())
            wc(1).start()

    loop(1, 16, block)
    gather(f)
    a_full[:, lanes_f] = a4[mine, f]

    def mq(r):
        xq = (xl + r // 2) % 2
        zq = quad * 2 + (z + r) % 2
        return send(a4.at[mine], a4.at[mine], mq_s.at[r], mq_r.at[r], feat=xq * 8 + zq)

    loop(1, 4, lambda r: mq(r).start())

    loop(1, 16, lambda r: m1(r).wait_recv())
    loop(0, 2, lambda h: wc(h).wait_recv())

    def layer_one(n):
        cols = pl.ds(pl.multiple_of(n * 256, 256), 256)
        weight = w1[:, :, :, :, cols].reshape(2048, 256)
        out = jnp.dot(a_full[...], weight, preferred_element_type=F32)
        pre[:, cols] = out
        hidden_ref[:, cols] = (out * sigmoid(out)).astype(BF16)

    loop(0, 4, layer_one)

    counts = cnt_ref[...]
    count_float = counts.astype(F32)
    col = lax.broadcasted_iota(jnp.int32, (SEEDS, ROWS), 1)
    table = jnp.zeros((SEEDS, ROWS), F32)
    for j in range(FAN2):
        table = table + jnp.where((nbr_ref[:, j:j + 1] == col) & (j < counts), 1.0, 0.0)
    hidden = hidden_ref[...]
    seed_hidden = hidden[:SEEDS]
    neigh = (jnp.dot(table.astype(BF16), hidden, preferred_element_type=F32) / count_float).astype(BF16)

    w2_load.wait()
    both = jnp.concatenate([seed_hidden, neigh], axis=1)
    upper_pre = jnp.dot(both, w2[...], preferred_element_type=F32)
    upper_sigma = sigmoid(upper_pre)
    upper_hidden = (upper_pre * upper_sigma).astype(BF16)
    logits = jnp.dot(upper_hidden, headp[...], preferred_element_type=F32)
    logits_ref[...] = logits[:, 0:CLASSES]
    cls = lax.broadcasted_iota(jnp.int32, (SEEDS, 128), 1)
    live = cls < CLASSES
    top = jnp.max(jnp.where(live, logits, -jnp.inf), axis=1, keepdims=True)
    expo = jnp.where(live, jnp.exp(jnp.where(live, logits - top, 0.0)), 0.0)
    probability = expo / jnp.sum(expo, axis=1, keepdims=True)
    one_hot = jnp.where(cls == lab_ref[...], 1.0, 0.0)
    grad_logits = ((probability - one_hot) / 256.0).astype(BF16)

    wide_left = lax.broadcasted_iota(jnp.int32, (SEEDS, 128), 1) < 64
    for hx in range(2):
        for q in range(4):
            lo = hx * 512 + q * 128
            s = seed_hidden[:, lo:lo + 128].astype(F32)
            n = neigh[:, lo:lo + 128].astype(F32)
            even = jnp.where(wide_left, s, pltpu.roll(n, 64, 1)).astype(BF16)
            odd = jnp.where(wide_left, pltpu.roll(s, 64, 1), n).astype(BF16)
            for other in range(2):
                p_send[other, q, :, hx * 256:hx * 256 + 128] = even
                p_send[other, q, :, hx * 256 + 128:hx * 256 + 256] = odd
            p_send[hx, q, :, 512:640] = upper_hidden[:, lo:lo + 128]
            p_send[hx, q, :, 640:768] = grad_logits

    def m2(r):
        to = feat_at(r)
        return send(p_send.at[to // 8, (to % 8) // 2], p_recv.at[f], m2_s.at[r], m2_r.at[r], feat=to)

    loop(1, 16, lambda r: m2(r).start())
    p_recv[f] = p_send[xl, quad]

    back_hidden = lax.dot_general(grad_logits, headp[...], NT, preferred_element_type=F32)
    slope_two = upper_sigma + upper_pre * upper_sigma * (1.0 - upper_sigma)
    grad_upper = (back_hidden * slope_two).astype(BF16)
    back_two = lax.dot_general(grad_upper, w2[...], NT, preferred_element_type=F32)
    back = jnp.concatenate([back_two[:, 0:WIDE], back_two[:, WIDE:2 * WIDE] / count_float], axis=0)
    high = back.astype(BF16)
    low = (back - high.astype(F32)).astype(BF16)
    eye = jnp.where(lax.broadcasted_iota(jnp.int32, (SEEDS, ROWS), 0) == col, 1.0, 0.0)
    spread = jnp.concatenate([eye, table, eye, table], axis=0)
    back_rows = lax.dot_general(
        spread.astype(BF16), jnp.concatenate([high, low], axis=0), TN, preferred_element_type=F32
    )
    for j in range(4):
        for h in range(2):
            lo = (2 * j if h == 0 else 2 * ((j + 2) % 4) + 1) * 128
            cols = slice(lo, lo + 128)
            grad_pre = (back_rows[:, cols] * silu_slope(pre[:, cols])).astype(BF16)
            g_send[j, 0:ROWS, h * 128:h * 128 + 128] = grad_pre
            g_send[j, ROWS:ROWS + SEEDS, h * 128:h * 128 + 128] = grad_upper[:, cols]

    def m3(r):
        to = feat_at(r)
        return send(g_send.at[(to // 8) * 2 + to % 2], g_recv.at[f], m3_s.at[r], m3_r.at[r], feat=to)

    loop(1, 16, lambda r: m3(r).start())
    g_recv[f] = g_send[mine]

    loop(1, 16, lambda r: m2(r).wait_recv())
    every = p_recv[...].reshape(16 * SEEDS, 768)
    head_part = lax.dot_general(every[:, 640:768], every[:, 512:640], TN, preferred_element_type=F32)
    hd_send[...] = head_part[0:32].astype(BF16)

    def m5(r):
        return send(hd_send, hd_recv.at[d], m5_s.at[r], m5_r.at[r], dp=dp_at(r))

    loop(1, 16, lambda r: m5(r).start())
    hd_recv[d] = hd_send[...]

    loop(1, 4, lambda r: mq(r).wait_recv())
    loop(1, 16, lambda r: m3(r).wait_recv())
    g_all = g_recv[...]
    a_all = jnp.concatenate([a4[m].reshape(16 * ROWS, 128) for m in range(4)], axis=1)
    part_one = lax.dot_general(g_all[:, 0:ROWS].reshape(16 * ROWS, 256), a_all, TN, preferred_element_type=F32)
    part_two = lax.dot_general(
        g_all[:, ROWS:ROWS + SEEDS].reshape(16 * SEEDS, 256), every[:, 0:512], TN, preferred_element_type=F32
    )
    for i in range(4):
        for m in range(4):
            z_send[i, m, 0] = part_one[i * 64:i * 64 + 64, m * 128:m * 128 + 128].astype(BF16)
            z_send[i, m, 1] = part_two[i * 64:i * 64 + 64, m * 128:m * 128 + 128].astype(BF16)

    def final(n):
        i, m = n // 4, n % 4
        to_f = (m // 2) * 8 + quad * 2 + m % 2
        to_d = ((mine + 2 * (i // 2)) % 4) * 4 + (i // 2) * 2 + i % 2
        own = (to_f == f) & (to_d == d)
        return own, send(z_send.at[i, m], z_recv.at[d], m4_s.at[n], m4_r.at[d], feat=to_f, dp=to_d)

    def final_start(n):
        own, copy = final(n)

        @pl.when(jnp.logical_not(own))
        def _():
            copy.start()

        @pl.when(own)
        def _():
            z_recv[d] = z_send[n // 4, n % 4]

    loop(0, 16, final_start)

    def m5_in(r):
        m5(r).wait_recv()

    loop(1, 16, m5_in)
    head_sum = jnp.sum(hd_recv[...].astype(F32), axis=0)
    head_sum = jnp.where(f % 2 == 1, pltpu.roll(head_sum, 64, 1), head_sum)
    ghead_ref[...] = head_sum.T[0:64, 0:CLASSES]

    source = (y + 2 * xh) % 4

    def final_in(n):
        own = (source == mine) & (n == d)

        @pl.when(jnp.logical_not(own))
        def _():
            send(z_send.at[0, 0], z_recv.at[n], m4_s.at[0], m4_r.at[n], feat=f, dp=d).wait_recv()

    loop(0, 16, final_in)
    grads = jnp.sum(z_recv[...].astype(F32), axis=0)
    one_ref[...] = grads[0].T.reshape(2, 64, 64)
    two_ref[...] = grads[1].T.reshape(2, 64, 64)

    def left_all(r):
        wa(r).wait_send()
        m1(r).wait_send()
        m2(r).wait_send()
        m3(r).wait_send()
        m5(r).wait_send()

    loop(1, 16, left_all)
    for h in range(2):
        loop(1, 4, lambda r: wb(h, r).wait_send())
        wc(h).wait_send()
    loop(1, 4, lambda r: mq(r).wait_send())

    def final_left(n):
        own, copy = final(n)

        @pl.when(jnp.logical_not(own))
        def _():
            copy.wait_send()

    loop(0, 16, final_left)


def shards(
    node_feats, target_ids, layer_one_nbrs, layer_one_counts, layer_two_nbrs, layer_two_counts, labels,
    layer_one_weight, layer_two_weight, head_weight,
):
    one_counts = layer_one_counts[0]
    slots = jnp.arange(FAN1, dtype=jnp.int32)[:, None] < one_counts[None, :]
    picked = jnp.where(slots, layer_one_nbrs[0].T, NODES)
    idx = jnp.concatenate([target_ids, picked], axis=0)
    inv = 1.0 / one_counts.astype(F32)[None, :]
    vmem = pl.BlockSpec(memory_space=pltpu.VMEM)
    smem = pl.BlockSpec(memory_space=pltpu.SMEM)
    hbm = pl.BlockSpec(memory_space=pl.ANY)
    dma = pltpu.SemaphoreType.DMA
    hidden, logits, grad_one, grad_two, grad_head = pl.pallas_call(
        kernel,
        out_shape=(
            jax.ShapeDtypeStruct((ROWS, WIDE), BF16),
            jax.ShapeDtypeStruct((SEEDS, CLASSES), F32),
            jax.ShapeDtypeStruct((2, 64, 64), F32),
            jax.ShapeDtypeStruct((2, 64, 64), F32),
            jax.ShapeDtypeStruct((64, CLASSES), F32),
        ),
        in_specs=[smem, smem, hbm, hbm, hbm, vmem, vmem, vmem, vmem],
        out_specs=(vmem,) * 5,
        scratch_shapes=[
            pltpu.VMEM((NODES, 64), BF16),
            pltpu.VMEM((NODES + 8, 128), F32),
            pltpu.VMEM((ROWS, 128), F32),
            pltpu.VMEM((4, 16, ROWS, 128), BF16),
            pltpu.VMEM((ROWS, 2048), BF16),
            pltpu.VMEM((16, 4, 2, 16, WIDE), BF16),
            pltpu.VMEM((2 * WIDE, WIDE), BF16),
            pltpu.VMEM((WIDE, 128), BF16),
            pltpu.VMEM((ROWS, WIDE), F32),
            pltpu.VMEM((2, 4, SEEDS, 768), BF16),
            pltpu.VMEM((16, SEEDS, 768), BF16),
            pltpu.VMEM((4, ROWS + SEEDS, 256), BF16),
            pltpu.VMEM((16, ROWS + SEEDS, 256), BF16),
            pltpu.VMEM((4, 4, 2, 64, 128), BF16),
            pltpu.VMEM((16, 2, 64, 128), BF16),
            pltpu.VMEM((32, 128), BF16),
            pltpu.VMEM((16, 32, 128), BF16),
            dma((3,)),
            dma((16,)), dma((16,)),
            dma((2, 4)), dma((2, 4)),
            dma((2,)), dma((2,)),
            dma((16,)), dma((16,)),
            dma((4,)), dma((4,)),
            dma((16,)), dma((16,)),
            dma((16,)), dma((16,)),
            dma((16,)), dma((16,)),
            dma((16,)), dma((16,)),
        ],
        compiler_params=pltpu.CompilerParams(
            collective_id=0, has_side_effects=True, vmem_limit_bytes=48 * 1024 * 1024
        ),
        name="step",
    )(
        idx, inv, node_feats[0], layer_one_weight.reshape(4, 2, 16, WIDE), layer_two_weight.reshape(2 * WIDE, WIDE),
        head_weight, layer_two_nbrs[0], layer_two_counts.reshape(SEEDS, 1), labels.reshape(SEEDS, 1),
    )
    return hidden[None], logits[None], grad_one, grad_two, grad_head


def solution(mesh):
    return jax.shard_map(
        shards,
        mesh=mesh,
        in_specs=(
            P("dp", None, "feat"),
            P("dp", None),
            P("dp", None, None),
            P("dp", None),
            P("dp", "feat", None),
            P("dp", "feat"),
            P("dp", "feat"),
            P(None, "feat", None),
            P(),
            P(),
        ),
        out_specs=(
            P("dp", "feat", None),
            P("dp", "feat", None),
            P(None, "feat", "dp"),
            P(None, "feat", "dp"),
            P("feat", None),
        ),
        check_vma=False,
    )
```

time: 563 us -> 120 us (0.21)
  waiting for transfers between devices: 360 us -> 0 us
  Pallas kernels: 0 us -> 106 us
  blocking collectives: 71.8 us -> 0 us
  local copies, waits for them, and re-layouts: 76.8 us -> 9.15 us
  other arithmetic: 20.8 us -> 2.97 us
  matrix products: 16.7 us -> 0 us
  between operations: 14.4 us -> 0.67 us
    unnamed x9 -> x0, waiting for transfers between devices: 149 us -> none
    reduce_scatter x2 -> x0, waiting for transfers between devices: 144 us -> none  [the longest x1 73.4 us: shards(): lax.psum_scatter(grad_two.astype(jnp.bfloat16), 'feat', scatter_dimension...]
    pallas_call x0 -> x1, Pallas kernels: none -> 106 us  [shards(): pl.pallas_call(kernel, out_shape=(jax.ShapeDtypeStruct((ROWS, WIDE), BF16...]
    psum x1 -> x0, blocking collectives: 71.8 us -> none  [shards(): grad_head_out = lax.psum(head_part, 'dp')]
    all_gather x1 -> x0, waiting for transfers between devices: 67 us -> none  [shards(): piece = lax.all_gather(grad_pre, 'feat', axis=0, tiled=True)]
    gather x5 -> x0, local copies, waits for them, and re-layouts: 66.4 us -> none  [the longest x2 62.4 us: shards(): picked_one = jnp.take(features, layer_one_nbrs[0], axis=0)]
    dot_general x14 -> x0, matrix products: 16.7 us -> none  [the longest x1 3.01 us: shards(): jnp.einsum('rc,rh->ch', part_mean, piece, preferred_element_type=jnp.floa...]
    reduce_sum x4 -> x0, other arithmetic: 11 us -> none  [the longest x1 10.4 us: shards(): jnp.sum(jnp.where(valid_one[:, :, None], picked_one, jnp.zeros((), jnp.bf...]
  transfers between devices with their start and end apart: 6 -> 0, of which waited for: 6 -> 0; matrix products, arithmetic and copies ran while one was open for 3% -> 0% of each run, Pallas kernels for 0% -> 0%
where the time goes in v1:
time: 120 us; the launch traced here: 119 us
  Pallas kernels  106 us (88%)
  local copies, waits for them, and re-layouts  9.15 us (8%)
  other arithmetic  2.97 us (2%)
    pallas_call x1, Pallas kernels, shards(): pl.pallas_call(kernel, out_shape=(jax.ShapeDtypeStruct((ROWS, WIDE), BF16...  106 us
    unnamed x9, local copies, waits for them, and re-layouts  6.92 us

profile of v1, /device:TPU:1, one launch (start us, length us, event | category | flops | bytes accessed | tf_op | source)
XLA Modules:
  0.0 119.3 jit_solution(4138432613206659799)
XLA Ops:
  0.6 0.7 convert_divide_fusion.inv_ref
  1.3 0.8 copy.21
  2.1 0.7 copy.18.cnt_ref
  2.8 0.7 copy.19.lab_ref
  3.6 0.7 reduce
  4.3 0.8 bitcast_select_fusion
  5.1 0.7 pad_add_fusion.idx_ref
  5.8 1.0 copy.16.head_ref
  6.8 1.8 %copy.15 = bf16[1,6144,64]{2,1,0:T(8,128)(2,1)S(1)} copy(bf16[1,6144,64]{1,2,0:T(8,128)(2,1)} %param.10) | data formatting | bytes 1572864 | tf_op args[0]
  8.6 0.0 copy-start
  8.6 0.9 copy-done
  9.6 106.5 %step.1 = (bf16[96,1024]{1,0:T(8,128)(2,1)S(1)}, f32[16,19]{1,0:T(8,128)S(1)}, f32[2,64,64]{2,1,0:T(8,128)S(1)}, f32[2,64,64]{2,1,0:T(8,128)S(1)}, f32[64,19]{1,0:T(8,128)S(1)}) custom-call(s32[11,1536]{1,0:T(8,128)S(1)} %pad_add_fusion.idx_ref, f32[1,1536]{1,0:T(1,128)S(1)} %convert_divide_fusion.inv_ref, bf16[6144,64]{1,0:T(8,128)(2,1)S(1)} %bitcast.12, ...), custom_call_target="tpu_custom_call" | custom-call | tf_op jit(solution)/shard_map/step/pallas_call | solution.py:360
  116.0 0.7 copy.20
  116.7 0.7 copy.28
  117.4 0.6 copy.29
  118.0 0.6 copy.30
  118.6 0.6 copy.31
Async XLA Ops:
  8.6 1.0 copy-start

commit v2 on v1

v2 whole, which is shorter than its diff:
```python
import functools

import jax
import jax.numpy as jnp
from jax import lax
from jax.experimental import pallas as pl
from jax.experimental.pallas import tpu as pltpu
from jax.sharding import PartitionSpec as P

MESH = pl.DeviceIdType.MESH
BF16 = jnp.bfloat16
F32 = jnp.float32

NODES = 6144
ROWS = 96
SEEDS = 16
FAN1 = 10
FAN2 = 5
CLASSES = 19
WIDE = 1024
WB0, WB1, WC0, WC1 = 3, 8, 12, 15
TN = (((0,), (0,)), ((), ()))
NT = (((1,), (1,)), ((), ()))


def sigmoid(values):
    return 1.0 / (1.0 + jnp.exp(-values))


def silu_slope(values):
    sigma = sigmoid(values)
    return sigma + values * sigma * (1.0 - sigma)


def kernel(
    self_ref, one_nbr_ref, one_cnt_ref, feats_hbm, w1_hbm, w2_hbm, head_ref, nbr_ref, cnt_ref, lab_ref,
    hidden_ref, logits_ref, one_ref, two_ref, ghead_ref,
    idx_vmem, idx_ref, inv_vmem, inv_ref, feats, tab, rows, a_send, a_pool, w1, w2, headp, pre,
    p_send, p_recv, sn_send, sn_pool, g_send, g_pool, gu_all, x1_send, x1_recv, z1_send, z1_recv, x2_send, x2_recv,
    hd_send, hd_recv,
    load_sem, wa_s, wa_r, wb_s, wb_r, wx_s, wx_r, wc_s, wc_r, m1_s, m1_r, ma_s, ma_r, ms_s, ms_r, m2_s, m2_r,
    sz_s, sz_r, sy_s, sy_r, sc_s, sc_r, m3_s, m3_r, gz_s, gz_r, x1_s, x1_r, z1_s, z1_r, x2_s, x2_r, m5_s, m5_r,
):
    f = lax.axis_index("feat")
    d = lax.axis_index("dp")
    xl, z = f // 8, f % 8
    y, xh, c = d // 4, (d // 2) % 2, d % 2
    x = xh * 2 + xl
    quad = z // 2

    def feat_at(r):
        return ((xl + r // 8) % 2) * 8 + (z + r % 8) % 8

    def feat_from(r):
        return ((xl + r // 8) % 2) * 8 + (z + 8 - r % 8) % 8

    def z_at(r):
        return xl * 8 + (z + r) % 8

    def y_at(r):
        return ((y + r) % 4) * 4 + xh * 2 + c

    def x_at(r):
        to = (x + r) % 4
        return {"feat": (to % 2) * 8 + z, "dp": y * 4 + (to // 2) * 2 + c}

    def yc_at(r):
        return (y + r // 2) % 4, (c + r % 2) % 2

    sibling = y * 4 + xh * 2 + 1 - c

    def send(src, dst, ss, rs, **where):
        return pltpu.make_async_remote_copy(
            src_ref=src, dst_ref=dst, send_sem=ss, recv_sem=rs, device_id=where, device_id_type=MESH
        )

    def loop(lo, hi, fn):
        def body(i, carry):
            fn(i)
            return carry

        lax.fori_loop(lo, hi, body, 0)

    waits = {}

    def now(name):
        waits.pop(name)()

    def comm(name, lo, hi, make, start=True):
        if start:
            loop(lo, hi, lambda r: make(r).start())
        waits[name + "_s"] = lambda: loop(lo, hi, lambda r: make(r).wait_send())
        waits[name + "_r"] = lambda: loop(lo, hi, lambda r: make(r).wait_recv())

    barrier = pltpu.get_barrier_semaphore()

    def greet(r):
        pl.semaphore_signal(barrier, inc=1, device_id={"feat": feat_at(r)}, device_id_type=MESH)
        pl.semaphore_signal(barrier, inc=1, device_id={"dp": (d + r) % 16}, device_id_type=MESH)

    loop(1, 16, greet)
    corner = {"feat": (1 - xl) * 8 + z, "dp": y * 4 + (1 - xh) * 2 + c}
    pl.semaphore_signal(barrier, inc=1, device_id=corner, device_id_type=MESH)

    w1_load = pltpu.make_async_copy(w1_hbm.at[y, c], w1.at[xl, z, y, c], load_sem.at[2])
    w1_load.start()

    def feat_load(i):
        part = pl.ds(pl.multiple_of(i * 1024, 1024), 1024)
        return pltpu.make_async_copy(feats_hbm.at[:, part], feats.at[:, part], load_sem.at[4 + i])

    loop(0, 6, lambda i: feat_load(i).start())
    w2_load = pltpu.make_async_copy(w2_hbm, w2, load_sem.at[1])
    w2_load.start()
    waits["w2"] = lambda: w2_load.wait()

    one_counts = one_cnt_ref[...]
    for j in range(FAN1):
        idx_vmem[j] = jnp.where(j < one_counts, one_nbr_ref[j], NODES)
    inv_vmem[...] = 1.0 / one_counts.astype(F32)
    idx_load = pltpu.make_async_copy(idx_vmem, idx_ref, load_sem.at[0])
    idx_load.start()
    inv_load = pltpu.make_async_copy(inv_vmem, inv_ref, load_sem.at[3])
    inv_load.start()
    headp[...] = jnp.zeros_like(headp)
    headp[0:CLASSES, :] = head_ref[...]

    def wa(r):
        return send(w1.at[xl, z, y, c], w1.at[xl, z, y, c], wa_s.at[r], wa_r.at[r], feat=z_at(r))

    w1_load.wait()
    pl.semaphore_wait(barrier, 31)
    comm("wa", 1, 8, wa)

    def widen(i):
        feat_load(i).wait()

        def tile(t):
            first = pl.multiple_of(i * 1024 + t * 128, 128)
            part = feats[:, pl.ds(first, 128)].astype(F32)
            tab[pl.ds(first, 128), :] = jnp.concatenate([part, part], axis=0).T

        loop(0, 8, tile)

    loop(0, 6, widen)
    tab[pl.ds(NODES, 8), :] = jnp.zeros((8, 128), F32)
    idx_load.wait()
    inv_load.wait()

    def wb(g, r):
        spot = w1.at[xl, pl.ds(((xh + g) % 2) * 4, 4), y, c]
        return send(spot, spot, wb_s.at[g, r], wb_r.at[g, r], dp=y_at(r))

    def wx(n):
        r, s = n // 2, n % 2
        spot = w1.at[xl, pl.ds(xh * 4, 4), (y + 4 - r) % 4, c]
        return send(spot, spot, wx_s.at[n], wx_r.at[n], **x_at(1 + 2 * s))

    def wc(g):
        spot = w1.at[(xl + g) % 2, :, :, c]
        return send(spot, spot, wc_s.at[g], wc_r.at[g], dp=sibling)

    lane = lax.broadcasted_iota(jnp.int32, (1, 128), 1)
    left = lane < 64

    def gather(k):
        def body(g):
            for u in range(8):
                local = g * 8 + u
                t = k * ROWS + local
                own = tab[pl.ds(self_ref[0, t], 1), :]
                total = [tab[pl.ds(idx_ref[j, 0, t], 1), :] for j in range(FAN1)]
                while len(total) > 1:
                    total = [
                        total[i] + total[i + 1] if i + 1 < len(total) else total[i]
                        for i in range(0, len(total), 2)
                    ]
                rows[pl.ds(local, 1), :] = jnp.where(left, own, total[0] * inv_ref[0, t])

        loop(0, ROWS // 8, body)
        a_send[k] = rows[...].astype(BF16)

    def lanes(block):
        return pl.ds(pl.multiple_of(block * 128, 128), 128)

    def m1(r):
        return send(a_send.at[feat_at(r)], a_pool.at[y, c, :, lanes(f)], m1_s.at[r], m1_r.at[r], feat=feat_at(r))

    def ma(r, i):
        spot = a_pool.at[y, c, :, lanes(feat_from(r))]
        return send(spot, spot, ma_s.at[r, i], ma_r.at[i], dp=y_at(i))

    def pass_on(r):
        m1(r).wait_recv()
        loop(1, 4, lambda i: ma(r, i).start())

    def block(r):
        gather(feat_at(r))
        m1(r).start()

        @pl.when(r == WB0)
        def _():
            now("wa_r")
            loop(1, 4, lambda i: wb(0, i).start())
            loop(0, 2, lambda n: wx(n).start())

        @pl.when(r == WB1)
        def _():
            loop(1, 4, lambda i: wb(0, i).wait_recv())
            loop(2, 8, lambda n: wx(n).start())
            loop(1, 4, lambda i: wb(1, i).start())

        @pl.when(r >= 9)
        def _():
            pass_on(2 * r - 17)
            pass_on(2 * r - 16)

        @pl.when(r == WC0)
        def _():
            loop(1, 4, lambda i: wb(1, i).wait_recv())
            wc(0).start()

        @pl.when(r == WC1)
        def _():
            loop(0, 8, lambda n: wx(n).wait_recv())
            wc(1).start()

    loop(1, 16, block)
    waits["wb_s"] = lambda: [loop(1, 4, lambda r, g=g: wb(g, r).wait_send()) for g in range(2)]
    comm("wc", 0, 2, wc, False)
    waits["wx_s"] = lambda: loop(0, 8, lambda n: wx(n).wait_send())
    waits["m1_s"] = lambda: loop(1, 16, lambda r: m1(r).wait_send())
    gather(f)
    a_pool[y, c, :, lanes(f)] = a_send[f]
    loop(1, 4, lambda i: ma(0, i).start())
    pass_on(15)
    waits["ma_s"] = lambda: loop(0, 16, lambda r: loop(1, 4, lambda i: ma(r, i).wait_send()))

    def ma_wait(i):
        send(a_pool.at[y, c], a_pool.at[y, c], ma_s.at[0, i], ma_r.at[i], dp=y_at(i)).wait_recv()

    waits["ma_r"] = lambda: loop(1, 4, ma_wait)
    now("wc_r")

    def layer_one(n):
        cols = pl.ds(pl.multiple_of(n * 256, 256), 256)
        weight = w1[:, :, :, :, :, cols].reshape(2048, 256)
        out = jnp.dot(a_pool[y, c], weight, preferred_element_type=F32)
        pre[:, cols] = out
        hidden_ref[:, cols] = (out * sigmoid(out)).astype(BF16)

    loop(0, 4, layer_one)

    eye = lax.broadcasted_iota(jnp.int32, (SEEDS, SEEDS), 0) == lax.broadcasted_iota(jnp.int32, (SEEDS, SEEDS), 1)

    def column(row):
        return jnp.sum(jnp.where(eye, row, 0), axis=1, keepdims=True)

    counts = column(cnt_ref[...])
    count_float = counts.astype(F32)
    col = lax.broadcasted_iota(jnp.int32, (SEEDS, ROWS), 1)
    table = jnp.zeros((SEEDS, ROWS), F32)
    for j in range(FAN2):
        table = table + jnp.where((column(nbr_ref[j]) == col) & (j < counts), 1.0, 0.0)
    hidden = hidden_ref[...]
    seed_hidden = hidden[:SEEDS]
    neigh = (jnp.dot(table.astype(BF16), hidden, preferred_element_type=F32) / count_float).astype(BF16)

    wide_left = lax.broadcasted_iota(jnp.int32, (SEEDS, 128), 1) < 64
    for hx in range(2):
        for q in range(4):
            lo = hx * 512 + q * 128
            s = seed_hidden[:, lo:lo + 128].astype(F32)
            n = neigh[:, lo:lo + 128].astype(F32)
            here = slice(hx * 128, hx * 128 + 128)
            sn_send[2 * q, :, here] = jnp.where(wide_left, s, pltpu.roll(n, 64, 1)).astype(BF16)
            sn_send[2 * q + 1, :, here] = jnp.where(wide_left, pltpu.roll(s, 64, 1), n).astype(BF16)

    def sz(r):
        return send(sn_send.at[(z + r) % 8], sn_pool.at[z, y, c], sz_s.at[r], sz_r.at[r], feat=z_at(r))

    comm("sz", 1, 8, sz)
    sn_pool[z, y, c] = sn_send[z]

    now("w2")
    both = jnp.concatenate([seed_hidden, neigh], axis=1)
    upper_pre = jnp.dot(both, w2[...], preferred_element_type=F32)
    upper_sigma = sigmoid(upper_pre)
    upper_hidden = (upper_pre * upper_sigma).astype(BF16)
    logits = lax.dot_general(upper_hidden, headp[...], NT, preferred_element_type=F32)
    logits_ref[...] = logits[:, 0:CLASSES]
    cls = lax.broadcasted_iota(jnp.int32, (SEEDS, 128), 1)
    live = cls < CLASSES
    top = jnp.max(jnp.where(live, logits, -jnp.inf), axis=1, keepdims=True)
    expo = jnp.where(live, jnp.exp(jnp.where(live, logits - top, 0.0)), 0.0)
    probability = expo / jnp.sum(expo, axis=1, keepdims=True)
    one_hot = jnp.where(cls == column(lab_ref[...]), 1.0, 0.0)
    grad_logits = ((probability - one_hot) / 256.0).astype(BF16)

    for hx in range(2):
        for q in range(4):
            lo = hx * 512 + q * 128
            p_send[hx, q, :, 0:128] = upper_hidden[:, lo:lo + 128]
            p_send[hx, q, :, 128:256] = grad_logits

    def m2(r):
        to = feat_at(r)
        return send(p_send.at[to // 8, (to % 8) // 2], p_recv.at[f], m2_s.at[r], m2_r.at[r], feat=to)

    comm("m2", 1, 16, m2)
    p_recv[f] = p_send[xl, quad]

    back_hidden = jnp.dot(grad_logits, headp[...], preferred_element_type=F32)
    slope_two = upper_sigma + upper_pre * upper_sigma * (1.0 - upper_sigma)
    grad_upper = (back_hidden * slope_two).astype(BF16)
    back_two = lax.dot_general(grad_upper, w2[...], NT, preferred_element_type=F32)
    back = jnp.concatenate([back_two[:, 0:WIDE], back_two[:, WIDE:2 * WIDE] / count_float], axis=0)
    high = back.astype(BF16)
    low = (back - high.astype(F32)).astype(BF16)
    first = jnp.where(lax.broadcasted_iota(jnp.int32, (SEEDS, ROWS), 0) == col, 1.0, 0.0)
    spread = jnp.concatenate([first, table, first, table], axis=0)
    back_rows = lax.dot_general(
        spread.astype(BF16), jnp.concatenate([high, low], axis=0), TN, preferred_element_type=F32
    )
    tall_left = lax.broadcasted_iota(jnp.int32, (ROWS + SEEDS, 128), 1) < 64
    for to_y in range(4):
        half = []
        for to_x in range(2):
            cols = slice(to_y * 256 + to_x * 128, to_y * 256 + to_x * 128 + 128)
            grad_pre = back_rows[:, cols] * silu_slope(pre[:, cols])
            half.append(jnp.concatenate([grad_pre, grad_upper[:, cols].astype(F32)], axis=0))
        g_send[to_y, 0] = jnp.where(tall_left, half[0], pltpu.roll(half[1], 64, 1)).astype(BF16)
        g_send[to_y, 1] = jnp.where(tall_left, pltpu.roll(half[0], 64, 1), half[1]).astype(BF16)

    def m3(r):
        to_y, to_c = yc_at(r)
        return send(
            g_send.at[to_y, to_c], g_pool.at[y, c], m3_s.at[r], m3_r.at[r], dp=to_y * 4 + xh * 2 + to_c
        )

    comm("m3", 1, 8, m3)
    g_pool[y, c] = g_send[y, c]

    def ms(n):
        spot = a_pool.at[:, c]
        return send(spot, spot, ms_s.at[n], ms_r.at[n], dp=sibling)

    now("ma_r")
    comm("ms", 0, 1, ms)

    def sy(r):
        spot = sn_pool.at[:, y, c]
        return send(spot, spot, sy_s.at[r], sy_r.at[r], dp=y_at(r))

    def sc(n):
        spot = sn_pool.at[:, :, c]
        return send(spot, spot, sc_s.at[n], sc_r.at[n], dp=sibling)

    now("sz_r")
    comm("sy", 1, 4, sy)

    now("m3_r")
    gu_all[z] = g_pool[:, :, ROWS:ROWS + SEEDS]

    def gz(r):
        return send(gu_all.at[z], gu_all.at[z], gz_s.at[r], gz_r.at[r], feat=z_at(r))

    comm("gz", 1, 8, gz)

    now("ms_r")
    part_one = lax.dot_general(
        g_pool[:, :, 0:ROWS].reshape(8 * ROWS, 128), a_pool[...].reshape(8 * ROWS, 2048), TN,
        preferred_element_type=F32,
    ).astype(BF16)
    for to_h in range(2):
        for to_l in range(2):
            x1_send[to_h, to_l] = part_one[to_h * 64:to_h * 64 + 64, to_l * 1024:to_l * 1024 + 1024]

    def x1(r):
        to = (x + r) % 4
        return send(x1_send.at[to // 2, to % 2], x1_recv.at[x], x1_s.at[r], x1_r.at[r], **x_at(r))

    comm("x1", 1, 4, x1)
    x1_recv[x] = x1_send[xh, xl]

    now("sy_r")
    comm("sc", 0, 1, sc)
    now("m2_r")
    every = p_recv[...].reshape(16 * SEEDS, 256)
    head_part = lax.dot_general(every[:, 128:256], every[:, 0:128], TN, preferred_element_type=F32)
    hd_send[...] = head_part[0:32].astype(BF16)

    def m5(r):
        return send(hd_send, hd_recv.at[d], m5_s.at[r], m5_r.at[r], dp=(d + r) % 16)

    comm("m5", 1, 16, m5)
    hd_recv[d] = hd_send[...]

    now("sc_r")
    now("gz_r")
    part_two = lax.dot_general(
        gu_all[...].reshape(64 * SEEDS, 128), sn_pool[...].reshape(64 * SEEDS, 256), TN, preferred_element_type=F32
    ).astype(BF16)
    for to_h in range(2):
        for to_l in range(2):
            x2_send[to_h, to_l] = part_two[to_h * 64:to_h * 64 + 64, to_l * 128:to_l * 128 + 128]

    def x2(r):
        to = (x + r) % 4
        return send(x2_send.at[to // 2, to % 2], x2_recv.at[x], x2_s.at[r], x2_r.at[r], **x_at(r))

    comm("x2", 1, 4, x2)
    x2_recv[x] = x2_send[xh, xl]

    now("x1_r")
    sum_x = jnp.sum(x1_recv[...].astype(F32), axis=0).astype(BF16)
    for to_z in range(8):
        z1_send[to_z] = sum_x[:, to_z * 128:to_z * 128 + 128]

    def z1(r):
        return send(z1_send.at[(z + r) % 8], z1_recv.at[z], z1_s.at[r], z1_r.at[r], feat=z_at(r))

    comm("z1", 1, 8, z1)
    z1_recv[z] = z1_send[z]

    now("m5_r")
    head_sum = jnp.sum(hd_recv[...].astype(F32), axis=0)
    head_sum = jnp.where(f % 2 == 1, pltpu.roll(head_sum, 64, 1), head_sum)
    ghead_ref[...] = head_sum[0:CLASSES, 0:64]

    now("x2_r")
    two_ref[...] = jnp.sum(x2_recv[...].astype(F32), axis=0).T.reshape(2, 64, 64)
    now("z1_r")
    one_ref[...] = jnp.sum(z1_recv[...].astype(F32), axis=0).T.reshape(2, 64, 64)

    for wait in waits.values():
        wait()


def shards(
    node_feats, target_ids, layer_one_nbrs, layer_one_counts, layer_two_nbrs, layer_two_counts, labels,
    layer_one_weight, layer_two_weight, head_weight,
):
    vmem = pl.BlockSpec(memory_space=pltpu.VMEM)
    smem = pl.BlockSpec(memory_space=pltpu.SMEM)
    hbm = pl.BlockSpec(memory_space=pltpu.HBM)
    dma = pltpu.SemaphoreType.DMA
    hidden, logits, grad_one, grad_two, grad_head = pl.pallas_call(
        kernel,
        out_shape=(
            jax.ShapeDtypeStruct((ROWS, WIDE), BF16),
            jax.ShapeDtypeStruct((SEEDS, CLASSES), F32),
            jax.ShapeDtypeStruct((2, 64, 64), F32),
            jax.ShapeDtypeStruct((2, 64, 64), F32),
            jax.ShapeDtypeStruct((CLASSES, 64), F32),
        ),
        in_specs=[smem, vmem, vmem, hbm, hbm, hbm, vmem, vmem, vmem, vmem],
        out_specs=(vmem,) * 5,
        scratch_shapes=[
            pltpu.VMEM((FAN1, 1, 16 * ROWS), jnp.int32),
            pltpu.SMEM((FAN1, 1, 16 * ROWS), jnp.int32),
            pltpu.VMEM((1, 16 * ROWS), F32),
            pltpu.SMEM((1, 16 * ROWS), F32),
            pltpu.VMEM((64, NODES), BF16),
            pltpu.VMEM((NODES + 8, 128), F32),
            pltpu.VMEM((ROWS, 128), F32),
            pltpu.VMEM((16, ROWS, 128), BF16),
            pltpu.VMEM((4, 2, ROWS, 2048), BF16),
            pltpu.VMEM((2, 8, 4, 2, 16, WIDE), BF16),
            pltpu.VMEM((2 * WIDE, WIDE), BF16),
            pltpu.VMEM((128, WIDE), BF16),
            pltpu.VMEM((ROWS, WIDE), F32),
            pltpu.VMEM((2, 4, SEEDS, 256), BF16),
            pltpu.VMEM((16, SEEDS, 256), BF16),
            pltpu.VMEM((8, SEEDS, 256), BF16),
            pltpu.VMEM((8, 4, 2, SEEDS, 256), BF16),
            pltpu.VMEM((4, 2, ROWS + SEEDS, 128), BF16),
            pltpu.VMEM((4, 2, ROWS + SEEDS, 128), BF16),
            pltpu.VMEM((8, 4, 2, SEEDS, 128), BF16),
            pltpu.VMEM((2, 2, 64, 1024), BF16),
            pltpu.VMEM((4, 64, 1024), BF16),
            pltpu.VMEM((8, 64, 128), BF16),
            pltpu.VMEM((8, 64, 128), BF16),
            pltpu.VMEM((2, 2, 64, 128), BF16),
            pltpu.VMEM((4, 64, 128), BF16),
            pltpu.VMEM((32, 128), BF16),
            pltpu.VMEM((16, 32, 128), BF16),
            dma((10,)),
            dma((8,)), dma((8,)),
            dma((2, 4)), dma((2, 4)),
            dma((8,)), dma((8,)),
            dma((2,)), dma((2,)),
            dma((16,)), dma((16,)),
            dma((16, 4)), dma((4,)),
            dma((1,)), dma((1,)),
            dma((16,)), dma((16,)),
            dma((8,)), dma((8,)),
            dma((4,)), dma((4,)),
            dma((1,)), dma((1,)),
            dma((8,)), dma((8,)),
            dma((8,)), dma((8,)),
            dma((4,)), dma((4,)),
            dma((8,)), dma((8,)),
            dma((4,)), dma((4,)),
            dma((16,)), dma((16,)),
        ],
        compiler_params=pltpu.CompilerParams(
            collective_id=0, has_side_effects=True, vmem_limit_bytes=60 * 1024 * 1024
        ),
        name="step",
    )(
        target_ids, layer_one_nbrs.transpose(2, 0, 1), layer_one_counts, node_feats[0].T,
        layer_one_weight.reshape(4, 2, 16, WIDE), layer_two_weight.reshape(2 * WIDE, WIDE), head_weight.T,
        layer_two_nbrs.transpose(2, 0, 1), layer_two_counts, labels,
    )
    return hidden[None], logits[None], grad_one, grad_two, grad_head.T


def solution(mesh):
    return jax.shard_map(
        shards,
        mesh=mesh,
        in_specs=(
            P("dp", None, "feat"),
            P("dp", None),
            P("dp", None, None),
            P("dp", None),
            P("dp", "feat", None),
            P("dp", "feat"),
            P("dp", "feat"),
            P(None, "feat", None),
            P(),
            P(),
        ),
        out_specs=(
            P("dp", "feat", None),
            P("dp", "feat", None),
            P(None, "feat", "dp"),
            P(None, "feat", "dp"),
            P("feat", None),
        ),
        check_vma=False,
    )
```

time: 120 us -> 85.5 us (0.71)
  Pallas kernels: 106 us -> 77.3 us
  other arithmetic: 2.97 us -> 0 us
  local copies, waits for them, and re-layouts: 9.15 us -> 7.16 us
    pallas_call x1, Pallas kernels: 106 us -> 77.3 us  [shards(): pl.pallas_call(kernel, out_shape=(jax.ShapeDtypeStruct((ROWS, WIDE), BF16...]
    reshape x2 -> x0, local copies, waits for them, and re-layouts: 1.46 us -> none  [the longest x1 0.73 us: shards(): layer_two_counts.reshape(SEEDS, 1)]
    unnamed x9 -> x5, local copies, waits for them, and re-layouts: 6.92 us -> 7.16 us
where the time goes in v2:
time: 85.5 us; the launch traced here: 85.1 us
  Pallas kernels  77.3 us (90%)
  local copies, waits for them, and re-layouts  7.16 us (8%)
    pallas_call x1, Pallas kernels, shards(): pl.pallas_call(kernel, out_shape=(jax.ShapeDtypeStruct((ROWS, WIDE), BF16...  77.3 us
    unnamed x5, local copies, waits for them, and re-layouts  7.16 us

profile of v2, /device:TPU:1, one launch (start us, length us, event | category | flops | bytes accessed | tf_op | source)
XLA Modules:
  0.0 85.1 jit_solution(16676945738460682709)
XLA Ops:
  0.6 77.3 %step.1 = (bf16[96,1024]{1,0:T(8,128)(2,1)}, f32[16,19]{1,0:T(8,128)}, f32[2,64,64]{2,1,0:T(8,128)}, f32[2,64,64]{2,1,0:T(8,128)}, f32[19,64]{1,0:T(8,128)}) custom-call(s32[1,1536]{1,0:T(1,128)} %self_ref.1, s32[10,1,1536]{2,1,0:T(1,128)} %bitcast.15, s32[1,1536]{1,0:T(1,128)} %one_cnt_ref.1, bf16[64,6144]{1,0:T(8,128)(2,1)} %bitcast.12, ...), custom_call_target="tpu_custom_call" | custom-call | tf_op jit(solution)/shard_map/step/pallas_call | solution.py:448
  78.0 1.6 %copy.20 = bf16[1,96,1024]{2,1,0:T(8,128)(2,1)} copy(bf16[1,96,1024]{2,1,0:T(8,128)(2,1)} %bitcast.14) | data formatting | bytes 393216
  79.6 1.3 %copy.21 = f32[1,16,19]{2,1,0:T(8,128)} copy(f32[1,16,19]{2,1,0:T(8,128)} %bitcast.18) | data formatting | bytes 2432
  80.9 1.5 %copy.22 = f32[2,64,64]{2,1,0:T(8,128)} copy(f32[2,64,64]{2,1,0:T(8,128)} %get-tuple-element.22) | data formatting | bytes 65536
  82.3 1.5 %copy.23 = f32[2,64,64]{2,1,0:T(8,128)} copy(f32[2,64,64]{2,1,0:T(8,128)} %get-tuple-element.23) | data formatting | bytes 65536
  83.8 1.3 %copy.24 = f32[64,19]{0,1:T(8,128)} copy(f32[64,19]{0,1:T(8,128)} %bitcast.17) | data formatting | bytes 9728

commit v3 on v2

v3 whole, which is shorter than its diff:
```python
import functools

import jax
import jax.numpy as jnp
from jax import lax
from jax.experimental import pallas as pl
from jax.experimental.pallas import tpu as pltpu
from jax.sharding import PartitionSpec as P

MESH = pl.DeviceIdType.MESH
BF16 = jnp.bfloat16
F32 = jnp.float32

NODES = 6144
ROWS = 96
TARGETS = 16 * ROWS
UNROLL = 16
SEEDS = 16
FAN1 = 10
FAN2 = 5
CLASSES = 19
WIDE = 1024
LAG, LAG_F, LAG_C, TO_X = 6, 9, 12, 13
TN = (((0,), (0,)), ((), ()))
NT = (((1,), (1,)), ((), ()))


def sigmoid(values):
    return 1.0 / (1.0 + jnp.exp(-values))


def silu_slope(values):
    sigma = sigmoid(values)
    return sigma + values * sigma * (1.0 - sigma)


def kernel(
    self_ref, one_nbr_ref, one_cnt_ref, feats_hbm, w1_hbm, w2_hbm, head_ref, nbr_ref, cnt_ref, lab_ref,
    hidden_ref, logits_ref, one_ref, two_ref, ghead_ref,
    idx_vmem, idx_ref, inv_vmem, inv_ref, feats, tab, rows, a_send, a_pool, w1, w2, headp, pre, h_send, hidden_vmem,
    p_send, p_recv, sn_send, sn_pool, b_send, b_pool, g_pool, gu_all, g_turned,
    x1_send, x1_recv, z1_send, z1_recv, x2_send, x2_recv, hd_send, hd_recv,
    load_sem, wa_s, wa_r, wx_s, wx_r, m1_s, m1_r, ma_s, ma_r, ms_s, ms_r, h_s, h_r, m2_s, m2_r,
    sz_s, sz_r, sy_s, sy_r, sc_s, sc_r, m3_s, m3_r, gz_s, gz_r, x1_s, x1_r, z1_s, z1_r, x2_s, x2_r, m5_s, m5_r,
):
    f = lax.axis_index("feat")
    d = lax.axis_index("dp")
    xl, z = f // 8, f % 8
    y, xh, c = d // 4, (d // 2) % 2, d % 2
    x = xh * 2 + xl
    quad = z // 2

    def feat_at(r):
        return ((xl + r // 8) % 2) * 8 + (z + r % 8) % 8

    def feat_from(r):
        return ((xl + r // 8) % 2) * 8 + (z + 8 - r % 8) % 8

    def z_at(r):
        return xl * 8 + (z + r) % 8

    def y_at(r):
        return ((y + r) % 4) * 4 + xh * 2 + c

    def x_at(r):
        to = (x + r) % 4
        return {"feat": (to % 2) * 8 + z, "dp": y * 4 + (to // 2) * 2 + c}

    def yc_at(r):
        return (y + r // 2) % 4, (c + r % 2) % 2

    sibling = y * 4 + xh * 2 + 1 - c

    def send(src, dst, ss, rs, **where):
        return pltpu.make_async_remote_copy(
            src_ref=src, dst_ref=dst, send_sem=ss, recv_sem=rs, device_id=where, device_id_type=MESH
        )

    def loop(lo, hi, fn):
        def body(i, carry):
            fn(i)
            return carry

        lax.fori_loop(lo, hi, body, 0)

    def lanes(block):
        return pl.ds(pl.multiple_of(block * 128, 128), 128)

    waits = {}

    def now(name):
        waits.pop(name)()

    def comm(name, lo, hi, make, start=True):
        if start:
            loop(lo, hi, lambda r: make(r).start())
        waits[name + "_s"] = lambda: loop(lo, hi, lambda r: make(r).wait_send())
        waits[name + "_r"] = lambda: loop(lo, hi, lambda r: make(r).wait_recv())

    barrier = pltpu.get_barrier_semaphore()

    def greet(r):
        pl.semaphore_signal(barrier, inc=1, device_id={"feat": feat_at(r)}, device_id_type=MESH)
        pl.semaphore_signal(barrier, inc=1, device_id={"dp": (d + r) % 16}, device_id_type=MESH)

    loop(1, 16, greet)
    for n in range(1, 4):
        corner = {"feat": (1 - xl) * 8 + z, "dp": y * 4 + ((xh + n // 2) % 2) * 2 + (c + n % 2) % 2}
        pl.semaphore_signal(barrier, inc=1, device_id=corner, device_id_type=MESH)

    w1_load = pltpu.make_async_copy(w1_hbm.at[:, lanes(y * 2 + c)], w1.at[xl, z], load_sem.at[2])
    w1_load.start()
    waits["w1"] = lambda: w1_load.wait()

    def feat_load(i):
        part = pl.ds(pl.multiple_of(i * 1024, 1024), 1024)
        return pltpu.make_async_copy(feats_hbm.at[:, part], feats.at[:, part], load_sem.at[4 + i])

    loop(0, 6, lambda i: feat_load(i).start())
    waits["feats"] = lambda: loop(0, 6, lambda i: feat_load(i).wait())
    w2_load = pltpu.make_async_copy(w2_hbm, w2, load_sem.at[1])
    w2_load.start()
    waits["w2"] = lambda: w2_load.wait()

    one_counts = one_cnt_ref[...]
    for j in range(FAN1):
        idx_vmem[:, j * TARGETS:(j + 1) * TARGETS] = jnp.where(j < one_counts, one_nbr_ref[j], NODES)
    inv_vmem[...] = 1.0 / one_counts.astype(F32)
    idx_load = pltpu.make_async_copy(idx_vmem, idx_ref, load_sem.at[0])
    idx_load.start()
    waits["idx"] = lambda: idx_load.wait()
    inv_load = pltpu.make_async_copy(inv_vmem, inv_ref, load_sem.at[3])
    inv_load.start()
    waits["inv"] = lambda: inv_load.wait()
    headp[...] = jnp.zeros_like(headp)
    headp[0:CLASSES, :] = head_ref[...]

    def wa(r):
        return send(w1.at[xl, z], w1.at[xl, z], wa_s.at[r], wa_r.at[r], feat=z_at(r))

    def wx(n):
        spot = w1.at[xl, pl.ds(xh * 4, 4)]
        return send(spot, spot, wx_s.at[n], wx_r.at[n], **x_at(1 + 2 * n))

    now("w1")
    pl.semaphore_wait(barrier, 33)
    comm("wa", 1, 8, wa)

    waits.pop("feats")

    for i in range(6):
        feat_load(i).wait()
        for first in range(i * 1024, i * 1024 + 1024, 128):
            part = feats[:, first:first + 128]
            tab[first:first + 128, :] = jnp.concatenate([part, part], axis=0).T.astype(F32)
    tab[pl.ds(NODES, 8), :] = jnp.zeros((8, 128), F32)
    now("idx")
    now("inv")

    lane = lax.broadcasted_iota(jnp.int32, (1, 128), 1)
    left = lane < 64

    def gather(k):
        def body(g):
            for u in range(UNROLL):
                local = g * UNROLL + u
                t = k * ROWS + local
                own = tab[pl.ds(self_ref[0, t], 1), :]
                total = [tab[pl.ds(idx_ref[0, j * TARGETS + t], 1), :] for j in range(FAN1)]
                while len(total) > 1:
                    total = [
                        total[i] + total[i + 1] if i + 1 < len(total) else total[i]
                        for i in range(0, len(total), 2)
                    ]
                rows[pl.ds(local, 1), :] = jnp.where(left, own, total[0] * inv_ref[0, t])

        loop(0, ROWS // UNROLL, body)
        a_send[k] = rows[...].astype(BF16)

    def m1(r):
        return send(a_send.at[feat_at(r)], a_pool.at[y, c, :, lanes(f)], m1_s.at[r], m1_r.at[r], feat=feat_at(r))

    def ma(r, i):
        spot = a_pool.at[y, c, :, lanes(feat_from(r))]
        return send(spot, spot, ma_s.at[r, i], ma_r.at[r, i], dp=y_at(i))

    def pass_two(step, r):
        after = 1 + 2 * (step % 2)
        ma(r, after).wait_recv()
        spot = a_pool.at[(y + 4 - after) % 4, c, :, lanes(feat_from(r))]
        return send(spot, spot, ma_s.at[r, 2], ma_r.at[r, 2], dp=y_at(after))

    def ma_wait(step, r):
        ma(r, 3 - 2 * (step % 2)).wait_recv()
        ma(r, 2).wait_recv()

    def ms(r):
        spot = a_pool.at[:, c, :, lanes(feat_from(r))]
        return send(spot, spot, ms_s.at[r], ms_r.at[0], dp=sibling)

    def pass_on(step):
        r = peer(step)
        m1(r).wait_recv()
        loop(0, 2, lambda i: ma(r, 1 + 2 * i).start())

    def forward(step):
        pass_two(step, peer(step)).start()

    def cross(step):
        r = peer(step)
        ma_wait(step, r)
        ms(r).start()

    def peer(step):
        t = step + 1
        far = 4 - t // 4
        sign, rx = (t % 4) // 2, (t + t // 16) % 2
        return rx * 8 + (far * (1 - sign) + (8 - far) * sign) % 8

    def block(step):
        r = peer(step)
        gather(feat_at(r))
        m1(r).start()
        pl.when(step > LAG)(lambda: pass_on(step - LAG))
        pl.when(step == LAG_F)(forward_own)
        pl.when(step > LAG_F)(lambda: forward(step - LAG_F))
        pl.when(step == LAG_C)(cross_own)
        pl.when(step > LAG_C)(lambda: cross(step - LAG_C))

        @pl.when(step == TO_X)
        def _():
            now("wa_r")
            loop(0, 2, lambda n: wx(n).start())

    def forward_own():
        pass_two(0, 0).start()

    def cross_own():
        ma_wait(0, 0)
        ms(0).start()

    gather(f)
    a_pool[y, c, :, lanes(f)] = a_send[f]
    loop(0, 2, lambda i: ma(0, 1 + 2 * i).start())
    loop(1, 16, block)
    comm("wx", 0, 2, wx, False)
    waits["m1_s"] = lambda: loop(1, 16, lambda r: m1(r).wait_send())
    loop(16 - LAG, 16, pass_on)
    waits["ma_s"] = lambda: loop(0, 16, lambda r: loop(1, 4, lambda i: ma(r, i).wait_send()))
    loop(16 - LAG_F, 16, forward)
    loop(16 - LAG_C, 16, cross)
    waits["ms_s"] = lambda: loop(0, 16, lambda r: ms(r).wait_send())

    def ms_all():
        send(a_pool.at[:, c], a_pool.at[:, c], ms_s.at[0], ms_r.at[0], dp=sibling).wait_recv()

    waits["ms_r"] = ms_all
    now("wx_r")
    now("ms_r")

    def hm(r):
        to_y, to_c = yc_at(r)
        return send(
            h_send.at[to_y, to_c], hidden_vmem.at[:, lanes(y * 2 + c)], h_s.at[r], h_r.at[r],
            dp=to_y * 4 + xh * 2 + to_c,
        )

    for q in (2, 1, 3, 0):
        to_y = (y + q) % 4
        out = jnp.dot(
            a_pool[to_y].reshape(2 * ROWS, 2048), w1[...].reshape(2048, 128), preferred_element_type=F32
        )
        pre[to_y] = out.reshape(2, ROWS, 128)
        h_send[to_y] = (out * sigmoid(out)).astype(BF16).reshape(2, ROWS, 128)
        for r in (2 * q, 2 * q + 1):
            if r:
                hm(r).start()
    comm("hm", 1, 8, hm, False)
    hidden_vmem[:, lanes(y * 2 + c)] = h_send[y, c]
    now("hm_r")
    hidden_out = pltpu.make_async_copy(hidden_vmem, hidden_ref, load_sem.at[14])
    hidden_out.start()
    waits["hidden"] = lambda: hidden_out.wait()

    eye = lax.broadcasted_iota(jnp.int32, (SEEDS, SEEDS), 0) == lax.broadcasted_iota(jnp.int32, (SEEDS, SEEDS), 1)

    def column(row):
        return jnp.sum(jnp.where(eye, row, 0), axis=1, keepdims=True)

    counts = column(cnt_ref[...])
    count_float = counts.astype(F32)
    col = lax.broadcasted_iota(jnp.int32, (SEEDS, ROWS), 1)
    table = jnp.zeros((SEEDS, ROWS), F32)
    for j in range(FAN2):
        table = table + jnp.where((column(nbr_ref[j]) == col) & (j < counts), 1.0, 0.0)
    hidden = hidden_vmem[...]
    seed_hidden = hidden[:SEEDS]
    neigh = (jnp.dot(table.astype(BF16), hidden, preferred_element_type=F32) / count_float).astype(BF16)

    wide_left = lax.broadcasted_iota(jnp.int32, (SEEDS, 128), 1) < 64
    for hx in range(2):
        for q in range(4):
            lo = hx * 512 + q * 128
            s = seed_hidden[:, lo:lo + 128].astype(F32)
            n = neigh[:, lo:lo + 128].astype(F32)
            here = slice(hx * 128, hx * 128 + 128)
            sn_send[2 * q, :, here] = jnp.where(wide_left, s, pltpu.roll(n, 64, 1)).astype(BF16)
            sn_send[2 * q + 1, :, here] = jnp.where(wide_left, pltpu.roll(s, 64, 1), n).astype(BF16)

    def sz(r):
        return send(sn_send.at[(z + r) % 8], sn_pool.at[z, y, c], sz_s.at[r], sz_r.at[r], feat=z_at(r))

    comm("sz", 1, 8, sz)
    sn_pool[z, y, c] = sn_send[z]

    now("w2")
    both = jnp.concatenate([seed_hidden, neigh], axis=1)
    upper_pre = jnp.dot(both, w2[...], preferred_element_type=F32)
    upper_sigma = sigmoid(upper_pre)
    upper_hidden = (upper_pre * upper_sigma).astype(BF16)
    logits = lax.dot_general(upper_hidden, headp[...], NT, preferred_element_type=F32)
    logits_ref[...] = logits[:, 0:CLASSES]
    cls = lax.broadcasted_iota(jnp.int32, (SEEDS, 128), 1)
    live = cls < CLASSES
    top = jnp.max(jnp.where(live, logits, -jnp.inf), axis=1, keepdims=True)
    expo = jnp.where(live, jnp.exp(jnp.where(live, logits - top, 0.0)), 0.0)
    probability = expo / jnp.sum(expo, axis=1, keepdims=True)
    one_hot = jnp.where(cls == column(lab_ref[...]), 1.0, 0.0)
    grad_logits = ((probability - one_hot) / 256.0).astype(BF16)

    for hx in range(2):
        for q in range(4):
            lo = hx * 512 + q * 128
            p_send[hx, q, :, 0:128] = upper_hidden[:, lo:lo + 128]
            p_send[hx, q, :, 128:256] = grad_logits

    def m2(r):
        to = feat_at(r)
        return send(p_send.at[to // 8, (to % 8) // 2], p_recv.at[f], m2_s.at[r], m2_r.at[r], feat=to)

    comm("m2", 1, 16, m2)
    p_recv[f] = p_send[xl, quad]

    back_hidden = jnp.dot(grad_logits, headp[...], preferred_element_type=F32)
    slope_two = upper_sigma + upper_pre * upper_sigma * (1.0 - upper_sigma)
    grad_upper = (back_hidden * slope_two).astype(BF16)
    back_two = lax.dot_general(grad_upper, w2[...], NT, preferred_element_type=F32)
    back = jnp.concatenate([back_two[:, 0:WIDE], back_two[:, WIDE:2 * WIDE] / count_float], axis=0)
    back = jnp.concatenate([back.astype(BF16), grad_upper], axis=0)
    wide_table = jnp.concatenate([table, jnp.zeros((SEEDS, 128 - ROWS), F32)], axis=1).astype(BF16)
    for e in range(8):
        b_send[e // 2, e % 2, 0:3 * SEEDS] = back[:, e * 128:e * 128 + 128]
        b_send[e // 2, e % 2, 3 * SEEDS:4 * SEEDS] = wide_table

    def m3(r):
        to_y, to_c = yc_at(r)
        return send(
            b_send.at[to_y, to_c], b_pool.at[y, c], m3_s.at[r], m3_r.at[r], dp=to_y * 4 + xh * 2 + to_c
        )

    comm("m3", 1, 8, m3)
    b_pool[y, c] = b_send[y, c]

    first = jnp.where(lax.broadcasted_iota(jnp.int32, (SEEDS, ROWS), 0) == col, 1.0, 0.0).astype(BF16)
    for r in range(8):
        if r:
            m3(r).wait_recv()
        at_y, at_c = (y + 4 - r // 2) % 4, (c + r) % 2
        terms = b_pool[at_y, at_c]
        spread = jnp.concatenate([first, terms[3 * SEEDS:4 * SEEDS, 0:ROWS]], axis=0)
        rows_back = lax.dot_general(spread, terms[0:2 * SEEDS], TN, preferred_element_type=F32)
        g_pool[at_y, at_c] = (rows_back * silu_slope(pre[at_y, at_c])).astype(BF16)
    waits.pop("m3_r")
    gu_all[z] = b_pool[:, :, 2 * SEEDS:3 * SEEDS]

    def gz(r):
        return send(gu_all.at[z], gu_all.at[z], gz_s.at[r], gz_r.at[r], feat=z_at(r))

    comm("gz", 1, 8, gz)

    g_turned[...] = g_pool[...].reshape(8 * ROWS, 128).T

    def to_final(n, src, dst, ss, rs):
        to_l, to_c = (xl + n // 2) % 2, (c + n % 2) % 2
        return send(src(to_c, to_l), dst(x), ss.at[n], rs.at[x], feat=to_l * 8 + z, dp=y * 4 + c * 2 + to_c)

    def final_start(src, dst, ss, rs):
        pl.when(xh != c)(lambda: to_final(0, src, dst, ss, rs).start())
        loop(1, 4, lambda n: to_final(n, src, dst, ss, rs).start())

        @pl.when(xh == c)
        def _():
            dst(x)[...] = src(c, xl)[...]

    def final_sent(src, dst, ss, rs):
        pl.when(xh != c)(lambda: to_final(0, src, dst, ss, rs).wait_send())
        loop(1, 4, lambda n: to_final(n, src, dst, ss, rs).wait_send())

    def final_came(src, dst, ss, rs):
        def came(n):
            @pl.when(jnp.logical_not((xh == c) & (n == x)))
            def _():
                send(src(0, 0), dst(n), ss.at[1], rs.at[n], feat=f, dp=d).wait_recv()

        loop(0, 4, came)

    def order(i):
        return 4 + (i // 2) * (1 - i % 2) - ((i + 1) // 2) * (i % 2)

    def x1(r):
        to_z = (z + r) % 8
        return (
            lambda to_c, to_l: x1_send.at[to_c, to_l, to_z],
            lambda n: x1_recv.at[n, to_z],
            x1_s.at[r],
            x1_r.at[r],
        )

    for i in range(8):
        to_z = (z + order(i)) % 8
        right = jnp.concatenate(
            [a_pool[:, :, :, lanes(to_z)].reshape(8 * ROWS, 128), a_pool[:, :, :, lanes(8 + to_z)].reshape(8 * ROWS, 128)],
            axis=1,
        )
        out = jnp.dot(g_turned[...], right, preferred_element_type=F32).astype(BF16)
        for to_c in range(2):
            for to_l in range(2):
                x1_send[to_c, to_l, to_z] = out[to_c * 64:to_c * 64 + 64, to_l * 128:to_l * 128 + 128]
        final_start(*x1(order(i)))
    waits["x1_s"] = lambda: loop(0, 8, lambda r: final_sent(*x1(r)))

    def sy(r):
        spot = sn_pool.at[:, y, c]
        return send(spot, spot, sy_s.at[r], sy_r.at[r], dp=y_at(r))

    def sc(n):
        spot = sn_pool.at[:, :, c]
        return send(spot, spot, sc_s.at[n], sc_r.at[n], dp=sibling)

    now("sz_r")
    comm("sy", 1, 4, sy)

    now("m2_r")
    every = p_recv[...].reshape(16 * SEEDS, 256)
    head_part = lax.dot_general(every[:, 128:256], every[:, 0:128], TN, preferred_element_type=F32)
    hd_send[...] = head_part[0:32].astype(BF16)

    def m5(r):
        return send(hd_send, hd_recv.at[d], m5_s.at[r], m5_r.at[r], dp=(d + r) % 16)

    comm("m5", 1, 16, m5)
    hd_recv[d] = hd_send[...]

    def z1(r):
        return send(z1_send.at[r], z1_recv.at[z], z1_s.at[r], z1_r.at[r], feat=z_at(r))

    def z1_start(i):
        r = order(i)
        final_came(*x1(r))
        z1_send[r] = jnp.sum(x1_recv[:, (z + r) % 8].astype(F32), axis=0).astype(BF16)
        pl.when(i < 7)(lambda: z1(r).start())

    loop(0, 8, z1_start)
    comm("z1", 1, 8, z1, False)
    z1_recv[z] = z1_send[0]

    now("sy_r")
    comm("sc", 0, 1, sc)
    now("gz_r")
    now("sc_r")
    part_two = lax.dot_general(
        gu_all[...].reshape(64 * SEEDS, 128), sn_pool[...].reshape(64 * SEEDS, 256), TN, preferred_element_type=F32
    ).astype(BF16)
    for to_c in range(2):
        for to_l in range(2):
            x2_send[to_c, to_l] = part_two[to_c * 64:to_c * 64 + 64, to_l * 128:to_l * 128 + 128]

    x2 = (lambda to_c, to_l: x2_send.at[to_c, to_l], lambda n: x2_recv.at[n], x2_s, x2_r)
    final_start(*x2)
    waits["x2_s"] = lambda: final_sent(*x2)
    waits["x2_r"] = lambda: final_came(*x2)

    now("m5_r")
    head_sum = jnp.sum(hd_recv[...].astype(F32), axis=0)
    head_sum = jnp.where(f % 2 == 1, pltpu.roll(head_sum, 64, 1), head_sum)
    ghead_ref[...] = head_sum[0:CLASSES, 0:64]

    now("x2_r")
    two_ref[...] = jnp.sum(x2_recv[...].astype(F32), axis=0).T.reshape(2, 64, 64)
    now("z1_r")
    one_ref[...] = jnp.sum(z1_recv[...].astype(F32), axis=0).T.reshape(2, 64, 64)

    for wait in waits.values():
        wait()


def finish(*refs):
    for i in range(5):
        refs[5 + i][...] = refs[i][...]


def shards(
    node_feats, target_ids, layer_one_nbrs, layer_one_counts, layer_two_nbrs, layer_two_counts, labels,
    layer_one_weight, layer_two_weight, head_weight,
):
    vmem = pl.BlockSpec(memory_space=pltpu.VMEM)
    smem = pl.BlockSpec(memory_space=pltpu.SMEM)
    hbm = pl.BlockSpec(memory_space=pltpu.HBM)
    dma = pltpu.SemaphoreType.DMA
    results = pl.pallas_call(
        kernel,
        out_shape=(
            jax.ShapeDtypeStruct((ROWS, WIDE), BF16),
            jax.ShapeDtypeStruct((SEEDS, CLASSES), F32),
            jax.ShapeDtypeStruct((2, 64, 64), F32),
            jax.ShapeDtypeStruct((2, 64, 64), F32),
            jax.ShapeDtypeStruct((CLASSES, 64), F32),
        ),
        in_specs=[smem, vmem, vmem, hbm, hbm, hbm, vmem, vmem, vmem, vmem],
        out_specs=(hbm, vmem, vmem, vmem, vmem),
        scratch_shapes=[
            pltpu.VMEM((1, FAN1 * TARGETS), jnp.int32),
            pltpu.SMEM((1, FAN1 * TARGETS), jnp.int32),
            pltpu.VMEM((1, TARGETS), F32),
            pltpu.SMEM((1, TARGETS), F32),
            pltpu.VMEM((64, NODES), BF16),
            pltpu.VMEM((NODES + 8, 128), F32),
            pltpu.VMEM((ROWS, 128), F32),
            pltpu.VMEM((16, ROWS, 128), BF16),
            pltpu.VMEM((4, 2, ROWS, 2048), BF16),
            pltpu.VMEM((2, 8, 128, 128), BF16),
            pltpu.VMEM((2 * WIDE, WIDE), BF16),
            pltpu.VMEM((128, WIDE), BF16),
            pltpu.VMEM((4, 2, ROWS, 128), F32),
            pltpu.VMEM((4, 2, ROWS, 128), BF16),
            pltpu.VMEM((ROWS, WIDE), BF16),
            pltpu.VMEM((2, 4, SEEDS, 256), BF16),
            pltpu.VMEM((16, SEEDS, 256), BF16),
            pltpu.VMEM((8, SEEDS, 256), BF16),
            pltpu.VMEM((8, 4, 2, SEEDS, 256), BF16),
            pltpu.VMEM((4, 2, 4 * SEEDS, 128), BF16),
            pltpu.VMEM((4, 2, 4 * SEEDS, 128), BF16),
            pltpu.VMEM((4, 2, ROWS, 128), BF16),
            pltpu.VMEM((8, 4, 2, SEEDS, 128), BF16),
            pltpu.VMEM((128, 8 * ROWS), BF16),
            pltpu.VMEM((2, 2, 8, 64, 128), BF16),
            pltpu.VMEM((4, 8, 64, 128), BF16),
            pltpu.VMEM((8, 64, 128), BF16),
            pltpu.VMEM((8, 64, 128), BF16),
            pltpu.VMEM((2, 2, 64, 128), BF16),
            pltpu.VMEM((4, 64, 128), BF16),
            pltpu.VMEM((32, 128), BF16),
            pltpu.VMEM((16, 32, 128), BF16),
            dma((15,)),
            dma((8,)), dma((8,)),
            dma((2,)), dma((2,)),
            dma((16,)), dma((16,)),
            dma((16, 4)), dma((16, 4)),
            dma((16,)), dma((1,)),
            dma((8,)), dma((8,)),
            dma((16,)), dma((16,)),
            dma((8,)), dma((8,)),
            dma((4,)), dma((4,)),
            dma((1,)), dma((1,)),
            dma((8,)), dma((8,)),
            dma((8,)), dma((8,)),
            dma((8, 4)), dma((8, 4)),
            dma((8,)), dma((8,)),
            dma((4,)), dma((4,)),
            dma((16,)), dma((16,)),
        ],
        compiler_params=pltpu.CompilerParams(
            collective_id=0, has_side_effects=True, vmem_limit_bytes=60 * 1024 * 1024
        ),
        name="step",
    )(
        target_ids, layer_one_nbrs.transpose(2, 0, 1), layer_one_counts, node_feats[0].T,
        layer_one_weight.reshape(128, WIDE), layer_two_weight.reshape(2 * WIDE, WIDE), head_weight.T,
        layer_two_nbrs.transpose(2, 0, 1), layer_two_counts, labels,
    )
    hidden, logits, grad_one, grad_two, grad_head = pl.pallas_call(
        finish,
        out_shape=tuple(jax.ShapeDtypeStruct(r.shape, r.dtype) for r in results),
        in_specs=[vmem] * 5,
        out_specs=(vmem,) * 5,
        name="finish",
    )(*results)
    return hidden[None], logits[None], grad_one, grad_two, grad_head.T


def solution(mesh):
    return jax.shard_map(
        shards,
        mesh=mesh,
        in_specs=(
            P("dp", None, "feat"),
            P("dp", None),
            P("dp", None, None),
            P("dp", None),
            P("dp", "feat", None),
            P("dp", "feat"),
            P("dp", "feat"),
            P(None, "feat", None),
            P(),
            P(),
        ),
        out_specs=(
            P("dp", "feat", None),
            P("dp", "feat", None),
            P(None, "feat", "dp"),
            P(None, "feat", "dp"),
            P("feat", None),
        ),
        check_vma=False,
    )
```

time: 85.5 us -> 80 us (0.936)
  local copies, waits for them, and re-layouts: 7.16 us -> 0 us
  Pallas kernels: 77.3 us -> 79.2 us
    unnamed x5 -> x0, local copies, waits for them, and re-layouts: 7.16 us -> none
    pallas_call x0 -> x1, Pallas kernels: none -> 1.71 us  [shards(): pl.pallas_call(finish, out_shape=tuple((jax.ShapeDtypeStruct(r.shape, r.d...]
where the time goes in v3:
time: 80 us; the launch traced here: 79.9 us
  Pallas kernels  79.2 us (99%)
    pallas_call x1, Pallas kernels, shards(): pl.pallas_call(kernel, out_shape=(jax.ShapeDtypeStruct((ROWS, WIDE), BF16...  77.5 us
    pallas_call x1, Pallas kernels, shards(): pl.pallas_call(finish, out_shape=tuple((jax.ShapeDtypeStruct(r.shape, r.d...  1.71 us

profile of v3, /device:TPU:1, one launch (start us, length us, event | category | flops | bytes accessed | tf_op | source)
XLA Modules:
  0.0 79.9 jit_solution(10732505419942040691)
XLA Ops:
  0.6 77.5 %step.1 = (bf16[96,1024]{1,0:T(8,128)(2,1)}, f32[16,19]{1,0:T(8,128)}, f32[2,64,64]{2,1,0:T(8,128)}, f32[2,64,64]{2,1,0:T(8,128)}, f32[19,64]{1,0:T(8,128)}) custom-call(s32[1,1536]{1,0:T(1,128)} %self_ref.1, s32[10,1,1536]{2,1,0:T(1,128)} %bitcast.14, s32[1,1536]{1,0:T(1,128)} %one_cnt_ref.1, bf16[64,6144]{1,0:T(8,128)(2,1)} %bitcast.12, ...), custom_call_target="tpu_custom_call" | custom-call | tf_op jit(solution)/shard_map/step/pallas_call | solution.py:510
  78.2 1.7 %finish.1 = (bf16[96,1024]{1,0:T(8,128)(2,1)}, f32[16,19]{1,0:T(8,128)}, f32[2,64,64]{2,1,0:T(8,128)}, f32[2,64,64]{2,1,0:T(8,128)}, f32[19,64]{1,0:T(8,128)}) custom-call(bf16[96,1024]{1,0:T(8,128)(2,1)} %get-tuple-element.15.refs_0_, f32[16,19]{1,0:T(8,128)} %get-tuple-element.16.refs_1_, f32[2,64,64]{2,1,0:T(8,128)} %get-tuple-element.17.refs_2_, ...), custom_call_target="tpu_custom_call" | custom-call | tf_op jit(solution)/shard_map/finish/pallas_call | solution.py:581

commit v4 on v3

--- a/solution.py
+++ b/solution.py
@@ -20,7 +20,11 @@
 FAN2 = 5
 CLASSES = 19
 WIDE = 1024
-LAG, LAG_F, LAG_C, TO_X = 6, 9, 12, 13
+SEQUENCE = (0, 8, 1, 7, 2, 6, 3, 5, 4, 12, 11, 13, 10, 14, 9, 15)
+DIRECT = (9, 15)
+TRAVEL = {0: 3.0, 1: 6.0, 2: 6.5, 3: 7.5, 4: 8.0}
+HOP = 3.0
+WX_STEP = 12.0
 TN = (((0,), (0,)), ((), ()))
 NT = (((1,), (1,)), ((), ()))
 
@@ -178,81 +182,70 @@
         a_send[k] = rows[...].astype(BF16)
 
     def m1(r):
-        return send(a_send.at[feat_at(r)], a_pool.at[y, c, :, lanes(f)], m1_s.at[r], m1_r.at[r], feat=feat_at(r))
+        return send(a_send.at[feat_at(r)], a_pool.at[f, y, c], m1_s.at[r], m1_r.at[r], feat=feat_at(r))
 
     def ma(r, i):
-        spot = a_pool.at[y, c, :, lanes(feat_from(r))]
+        spot = a_pool.at[feat_from(r), y, c]
         return send(spot, spot, ma_s.at[r, i], ma_r.at[r, i], dp=y_at(i))
 
-    def pass_two(step, r):
-        after = 1 + 2 * (step % 2)
-        ma(r, after).wait_recv()
-        spot = a_pool.at[(y + 4 - after) % 4, c, :, lanes(feat_from(r))]
+    def ma_two(place, r):
+        after = 1 + 2 * (place % 2)
+        spot = a_pool.at[feat_from(r), (y + 4 - after) % 4, c]
         return send(spot, spot, ma_s.at[r, 2], ma_r.at[r, 2], dp=y_at(after))
 
-    def ma_wait(step, r):
-        ma(r, 3 - 2 * (step % 2)).wait_recv()
-        ma(r, 2).wait_recv()
-
     def ms(r):
-        spot = a_pool.at[:, c, :, lanes(feat_from(r))]
+        spot = a_pool.at[feat_from(r), :, c]
         return send(spot, spot, ms_s.at[r], ms_r.at[0], dp=sibling)
 
-    def pass_on(step):
-        r = peer(step)
-        m1(r).wait_recv()
-        loop(0, 2, lambda i: ma(r, 1 + 2 * i).start())
-
-    def forward(step):
-        pass_two(step, peer(step)).start()
-
-    def cross(step):
-        r = peer(step)
-        ma_wait(step, r)
+    def pass_on(place, r):
+        if r:
+            m1(r).wait_recv()
+        for i in (1, 2, 3) if r in DIRECT else (1, 3):
+            ma(r, i).start()
+
+    def forward(place, r):
+        ma(r, 1 + 2 * (place % 2)).wait_recv()
+        ma_two(place, r).start()
+
+    def cross(place, r):
+        for i in (1, 2, 3) if r in DIRECT else (2, 3 - 2 * (place % 2)):
+            ma(r, i).wait_recv()
         ms(r).start()
 
-    def peer(step):
-        t = step + 1
-        far = 4 - t // 4
-        sign, rx = (t % 4) // 2, (t + t // 16) % 2
-        return rx * 8 + (far * (1 - sign) + (8 - far) * sign) % 8
-
-    def block(step):
-        r = peer(step)
+    def wx_start(place, r):
+        now("wa_r")
+        loop(0, 2, lambda n: wx(n).start())
+
+    events = [(WX_STEP, wx_start, 0, 0)]
+    for place, r in enumerate(SEQUENCE):
+        at = place + 1 + (TRAVEL[min(r % 8, 8 - r % 8)] if r else 0.0)
+        events.append((at, pass_on, place, r))
+        if r not in DIRECT:
+            at += HOP
+            events.append((at, forward, place, r))
+        events.append((at + HOP, cross, place, r))
+    events.sort(key=lambda event: event[0])
+
+    def run_events(until):
+        while events and events[0][0] <= until:
+            _, act, place, r = events.pop(0)
+            act(place, r)
+
+    for place, r in enumerate(SEQUENCE):
         gather(feat_at(r))
-        m1(r).start()
-        pl.when(step > LAG)(lambda: pass_on(step - LAG))
-        pl.when(step == LAG_F)(forward_own)
-        pl.when(step > LAG_F)(lambda: forward(step - LAG_F))
-        pl.when(step == LAG_C)(cross_own)
-        pl.when(step > LAG_C)(lambda: cross(step - LAG_C))
-
-        @pl.when(step == TO_X)
-        def _():
-            now("wa_r")
-            loop(0, 2, lambda n: wx(n).start())
-
-    def forward_own():
-        pass_two(0, 0).start()
-
-    def cross_own():
-        ma_wait(0, 0)
-        ms(0).start()
-
-    gather(f)
-    a_pool[y, c, :, lanes(f)] = a_send[f]
-    loop(0, 2, lambda i: ma(0, 1 + 2 * i).start())
-    loop(1, 16, block)
+        if r:
+            m1(r).start()
+        else:
+            a_pool[f, y, c] = a_send[f]
+        run_events(place + 1)
+    run_events(1000)
     comm("wx", 0, 2, wx, False)
     waits["m1_s"] = lambda: loop(1, 16, lambda r: m1(r).wait_send())
-    loop(16 - LAG, 16, pass_on)
     waits["ma_s"] = lambda: loop(0, 16, lambda r: loop(1, 4, lambda i: ma(r, i).wait_send()))
-    loop(16 - LAG_F, 16, forward)
-    loop(16 - LAG_C, 16, cross)
     waits["ms_s"] = lambda: loop(0, 16, lambda r: ms(r).wait_send())
 
     def ms_all():
-        send(a_pool.at[:, c], a_pool.at[:, c], ms_s.at[0], ms_r.at[0], dp=sibling).wait_recv()
+        send(a_pool.at[:, :, c], a_pool.at[:, :, c], ms_s.at[0], ms_r.at[0], dp=sibling).wait_recv()
 
     waits["ms_r"] = ms_all
     now("wx_r")
@@ -267,9 +260,8 @@
 
     for q in (2, 1, 3, 0):
         to_y = (y + q) % 4
-        out = jnp.dot(
-            a_pool[to_y].reshape(2 * ROWS, 2048), w1[...].reshape(2048, 128), preferred_element_type=F32
-        )
+        wide = jnp.concatenate([a_pool[b, to_y].reshape(2 * ROWS, 128) for b in range(16)], axis=1)
+        out = jnp.dot(wide, w1[...].reshape(2048, 128), preferred_element_type=F32)
         pre[to_y] = out.reshape(2, ROWS, 128)
         h_send[to_y] = (out * sigmoid(out)).astype(BF16).reshape(2, ROWS, 128)
         for r in (2 * q, 2 * q + 1):
@@ -419,7 +411,7 @@
     for i in range(8):
         to_z = (z + order(i)) % 8
         right = jnp.concatenate(
-            [a_pool[:, :, :, lanes(to_z)].reshape(8 * ROWS, 128), a_pool[:, :, :, lanes(8 + to_z)].reshape(8 * ROWS, 128)],
+            [a_pool[to_z].reshape(8 * ROWS, 128), a_pool[8 + to_z].reshape(8 * ROWS, 128)],
             axis=1,
         )
         out = jnp.dot(g_turned[...], right, preferred_element_type=F32).astype(BF16)
@@ -527,7 +519,7 @@
             pltpu.VMEM((NODES + 8, 128), F32),
             pltpu.VMEM((ROWS, 128), F32),
             pltpu.VMEM((16, ROWS, 128), BF16),
-            pltpu.VMEM((4, 2, ROWS, 2048), BF16),
+            pltpu.VMEM((16, 4, 2, ROWS, 128), BF16),
             pltpu.VMEM((2, 8, 128, 128), BF16),
             pltpu.VMEM((2 * WIDE, WIDE), BF16),
             pltpu.VMEM((128, WIDE), BF16),

time: 80 us -> 78 us (0.975)
  Pallas kernels: 79.2 us -> 77.2 us
    pallas_call x1, Pallas kernels: 77.5 us -> 75.5 us  [shards(): pl.pallas_call(kernel, out_shape=(jax.ShapeDtypeStruct((ROWS, WIDE), BF16...]
where the time goes in v4:
time: 78 us; the launch traced here: 77.9 us
  Pallas kernels  77.2 us (99%)
    pallas_call x1, Pallas kernels, shards(): pl.pallas_call(kernel, out_shape=(jax.ShapeDtypeStruct((ROWS, WIDE), BF16...  75.5 us
    pallas_call x1, Pallas kernels, shards(): pl.pallas_call(finish, out_shape=tuple((jax.ShapeDtypeStruct(r.shape, r.d...  1.71 us

profile of v4, /device:TPU:1, one launch (start us, length us, event | category | flops | bytes accessed | tf_op | source)
XLA Modules:
  0.0 77.9 jit_solution(6420222509724008377)
XLA Ops:
  0.6 75.5 %step.1 = (bf16[96,1024]{1,0:T(8,128)(2,1)}, f32[16,19]{1,0:T(8,128)}, f32[2,64,64]{2,1,0:T(8,128)}, f32[2,64,64]{2,1,0:T(8,128)}, f32[19,64]{1,0:T(8,128)}) custom-call(s32[1,1536]{1,0:T(1,128)} %self_ref.1, s32[10,1,1536]{2,1,0:T(1,128)} %bitcast.14, s32[1,1536]{1,0:T(1,128)} %one_cnt_ref.1, bf16[64,6144]{1,0:T(8,128)(2,1)} %bitcast.12, ...), custom_call_target="tpu_custom_call" | custom-call | tf_op jit(solution)/shard_map/step/pallas_call | solution.py:502
  76.2 1.7 %finish.1 = (bf16[96,1024]{1,0:T(8,128)(2,1)}, f32[16,19]{1,0:T(8,128)}, f32[2,64,64]{2,1,0:T(8,128)}, f32[2,64,64]{2,1,0:T(8,128)}, f32[19,64]{1,0:T(8,128)}) custom-call(bf16[96,1024]{1,0:T(8,128)(2,1)} %get-tuple-element.15.refs_0_, f32[16,19]{1,0:T(8,128)} %get-tuple-element.16.refs_1_, f32[2,64,64]{2,1,0:T(8,128)} %get-tuple-element.17.refs_2_, ...), custom_call_target="tpu_custom_call" | custom-call | tf_op jit(solution)/shard_map/finish/pallas_call | solution.py:573

commit v5 on v4

--- a/solution.py
+++ b/solution.py
@@ -432,17 +432,6 @@
     now("sz_r")
     comm("sy", 1, 4, sy)
 
-    now("m2_r")
-    every = p_recv[...].reshape(16 * SEEDS, 256)
-    head_part = lax.dot_general(every[:, 128:256], every[:, 0:128], TN, preferred_element_type=F32)
-    hd_send[...] = head_part[0:32].astype(BF16)
-
-    def m5(r):
-        return send(hd_send, hd_recv.at[d], m5_s.at[r], m5_r.at[r], dp=(d + r) % 16)
-
-    comm("m5", 1, 16, m5)
-    hd_recv[d] = hd_send[...]
-
     def z1(r):
         return send(z1_send.at[r], z1_recv.at[z], z1_s.at[r], z1_r.at[r], feat=z_at(r))
 
@@ -458,6 +447,18 @@
 
     now("sy_r")
     comm("sc", 0, 1, sc)
+
+    now("m2_r")
+    every = p_recv[...].reshape(16 * SEEDS, 256)
+    head_part = lax.dot_general(every[:, 128:256], every[:, 0:128], TN, preferred_element_type=F32)
+    hd_send[...] = head_part[0:32].astype(BF16)
+
+    def m5(r):
+        return send(hd_send, hd_recv.at[d], m5_s.at[r], m5_r.at[r], dp=(d + r) % 16)
+
+    comm("m5", 1, 16, m5)
+    hd_recv[d] = hd_send[...]
+
     now("gz_r")
     now("sc_r")
     part_two = lax.dot_general(

time: 78 us -> 78.8 us (1.010)
  Pallas kernels: 77.2 us -> 78 us
where the time goes in v5:
time: 78.8 us; the launch traced here: 78.6 us
  Pallas kernels  78 us (99%)
    pallas_call x1, Pallas kernels, shards(): pl.pallas_call(kernel, out_shape=(jax.ShapeDtypeStruct((ROWS, WIDE), BF16...  76.3 us
    pallas_call x1, Pallas kernels, shards(): pl.pallas_call(finish, out_shape=tuple((jax.ShapeDtypeStruct(r.shape, r.d...  1.71 us

profile of v5, /device:TPU:1, one launch (start us, length us, event | category | flops | bytes accessed | tf_op | source)
XLA Modules:
  0.0 78.6 jit_solution(13027594155170023913)
XLA Ops:
  0.6 76.3 %step.1 = (bf16[96,1024]{1,0:T(8,128)(2,1)}, f32[16,19]{1,0:T(8,128)}, f32[2,64,64]{2,1,0:T(8,128)}, f32[2,64,64]{2,1,0:T(8,128)}, f32[19,64]{1,0:T(8,128)}) custom-call(s32[1,1536]{1,0:T(1,128)} %self_ref.1, s32[10,1,1536]{2,1,0:T(1,128)} %bitcast.14, s32[1,1536]{1,0:T(1,128)} %one_cnt_ref.1, bf16[64,6144]{1,0:T(8,128)(2,1)} %bitcast.12, ...), custom_call_target="tpu_custom_call" | custom-call | tf_op jit(solution)/shard_map/step/pallas_call | solution.py:503
  76.9 1.7 %finish.1 = (bf16[96,1024]{1,0:T(8,128)(2,1)}, f32[16,19]{1,0:T(8,128)}, f32[2,64,64]{2,1,0:T(8,128)}, f32[2,64,64]{2,1,0:T(8,128)}, f32[19,64]{1,0:T(8,128)}) custom-call(bf16[96,1024]{1,0:T(8,128)(2,1)} %get-tuple-element.15.refs_0_, f32[16,19]{1,0:T(8,128)} %get-tuple-element.16.refs_1_, f32[2,64,64]{2,1,0:T(8,128)} %get-tuple-element.17.refs_2_, ...), custom_call_target="tpu_custom_call" | custom-call | tf_op jit(solution)/shard_map/finish/pallas_call | solution.py:574
